TPU v7x, 512 devices: a whole 4x8x8 slice. The times are simulated.
512 devices in a mesh: pipe: 32 (over y_hi, z), seq: 16 (over x, y_lo, core).
Axes of the slice: x: 4, y: 8 (y_hi: 4, y_lo: 2; y = y_hi * 2 + y_lo), z: 8, core: 2. Of those that a mesh axis runs over, the one named last changes fastest.
Arguments:
- activations: bfloat16 [32, 1024, 3072], P('pipe', 'seq'), may hold values from -6 to 6
- modulation: float32 [32, 3, 3072], P('pipe'), may hold values from -3 to 3
- w_qkv: bfloat16 [32, 3072, 3, 2048], P('pipe', None, None, 'seq'), may hold values from -0.109375 to 0.109375
- w_out: bfloat16 [32, 2048, 3072], P('pipe', None, 'seq'), may hold values from -0.125 to 0.125
- stale_kv: bfloat16 [32, 2, 1536, 2048], P('pipe', None, 'seq'), may hold values from -172 to 172
- section_micro: int32 [32], P('pipe'), may hold values from 0 to 3
- patch_micro: int32 [1536], replicated, may hold values from 0 to 3, as said below
Outputs:
- handed: bfloat16 [32, 1024, 3072], P('pipe', 'seq')
Inputs may be any that keep to these rules, and one draw needn't show every extreme that they name: `patch_micro`: each micro-batch index owns exactly 384 rows.
All inputs are finite; a program needn't handle non-finite values.
Results may differ from a plain program's by a relative error of at most 0.02.
The roundings to bfloat16 on the way count: a program that leaves them out, or rounds other values in their place, can miss the bound.
Values may be sent and summed in bfloat16 or wider, within the bound.
No kernel may reach another device: no remote copies, remote signals or barrier semaphores. Data moves between devices by JAX's collectives and lax.ppermute only.
A program may use at most 64 MiB of HBM per device.

v0:
```python
import jax
import jax.numpy as jnp
from jax import lax
from jax.sharding import PartitionSpec as P

HD = 128


def from_behind(value, axis, steps):
    count = lax.axis_size(axis)
    pairs = [(source, (source + steps) % count) for source in range(count)]
    return lax.ppermute(value, axis, pairs)


def normalize(rows, shift, scale):
    values = rows.astype(jnp.float32)
    mean = jnp.mean(values, axis=-1, keepdims=True)
    centred = values - mean
    var = jnp.mean(centred * centred, axis=-1, keepdims=True)
    normed = centred * lax.rsqrt(var + 1e-06)
    return (normed * (1.0 + scale) + shift).astype(jnp.bfloat16)


def attend_block(query, keys, values, keep_all):
    scores = jnp.einsum("qd,kd->qk", query, keys, preferred_element_type=jnp.float32) * HD ** (-0.5)
    scores = jnp.where(keep_all[None, :], scores, -jnp.inf)
    top = jnp.max(scores, axis=-1, keepdims=True)
    expo = jnp.exp(scores - top)
    weights = (expo / jnp.sum(expo, axis=-1, keepdims=True)).astype(jnp.bfloat16)
    return jnp.dot(weights, values, preferred_element_type=jnp.float32).astype(jnp.bfloat16)


def attend(query, keys, values, keep_all):
    total_rows = query.shape[0]
    block = min(512, total_rows)
    blocks = query.reshape(total_rows // block, block, query.shape[1])
    outcome = lax.map(lambda piece: attend_block(piece, keys, values, keep_all), blocks)
    return outcome.reshape(total_rows, values.shape[1])


def on_device(activations, modulation, w_qkv, w_out, stale_kv, section_micro, patch_micro):
    rows = activations[0]
    mod = modulation[0]
    width = rows.shape[1]
    columns = w_qkv.shape[3]
    heads_dev = columns // HD
    weight_in = w_qkv[0].reshape(width, 3 * columns)
    weight_out = w_out[0]
    hidden = normalize(rows, mod[0], mod[1])
    qkv = jnp.dot(
        lax.all_gather(hidden, "seq", axis=0, tiled=True),
        weight_in,
        preferred_element_type=jnp.float32,
    ).astype(jnp.bfloat16)
    micro_rows = qkv.shape[0]
    qkv = qkv.reshape(micro_rows, 3, heads_dev, HD)
    stale = lax.all_to_all(stale_kv[0], "seq", split_axis=2, concat_axis=1, tiled=True)
    stale_len = stale.shape[1]
    stale_heads = jnp.transpose(stale.reshape(2, stale_len, heads_dev, HD), (0, 2, 1, 3))
    keep_all = jnp.concatenate([jnp.ones((micro_rows,), bool), patch_micro != section_micro[0]])
    query = jnp.transpose(qkv[:, 0], (1, 0, 2))
    keys = jnp.concatenate([jnp.transpose(qkv[:, 1], (1, 0, 2)), stale_heads[0]], axis=1)
    values = jnp.concatenate([jnp.transpose(qkv[:, 2], (1, 0, 2)), stale_heads[1]], axis=1)
    heads = lax.map(lambda trio: attend(trio[0], trio[1], trio[2], keep_all), (query, keys, values))
    heads_out = jnp.transpose(heads, (1, 0, 2)).reshape(micro_rows, columns)
    projected = jnp.dot(
        lax.all_gather(heads_out, "seq", axis=1, tiled=True),
        weight_out,
        preferred_element_type=jnp.float32,
    )
    attn = lax.all_to_all(
        projected.astype(jnp.bfloat16), "seq", split_axis=0, concat_axis=1, tiled=True
    )
    section_out = (rows.astype(jnp.float32) + mod[2] * attn.astype(jnp.float32)).astype(
        jnp.bfloat16
    )
    result = from_behind(section_out, "pipe", 1)
    return result[None]


def solution(mesh):
    return jax.shard_map(
        on_device,
        mesh=mesh,
        in_specs=(
            P("pipe", "seq", None),
            P("pipe", None, None),
            P("pipe", None, None, "seq"),
            P("pipe", None, "seq"),
            P("pipe", None, "seq", None),
            P("pipe"),
            P(),
        ),
        out_specs=P("pipe", "seq", None),
        check_vma=False,
    )
```

profile of v0, /device:TPU:9, one launch (start us, length us, event | category | flops | bytes accessed | tf_op | source)
XLA Modules:
  0.0 188.4 jit_solution(10511919764973694500)
XLA Ops:
  7.4 1.2 convert_reduce_fusion
  8.5 1.3 fusion.12
  9.8 2.0 %fusion.15 = bf16[64,3072]{1,0:T(8,128)(2,1)} fusion(bf16[1,64,3072]{2,1,0:T(8,128)(2,1)} %param.9, f32[3072]{0:T(1024)S(1)} %bitcast.82, f32[3072]{0:T(1024)S(1)} %bitcast.83, f32[64]{0:T(128)S(1)} %add_rsqrt_fusion, f32[64]{0:T(128)S(1)} %broadcast_multiply_fusion), kind=kLoop, calls=%fused_computation.23 | loop fusion | flops 1179648 | bytes 811520 | tf_op jit(solution)/shard_map/convert_element_type | solution.py:21
  11.8 3.6 %copy.29 = bf16[1,2,96,2048]{2,1,3,0:T(2,128)(2,1)} copy(bf16[1,2,96,2048]{3,2,1,0:T(8,128)(2,1)} %param.13) | data formatting | bytes 1572864 | tf_op args[4]
  15.4 9.6 %all-to-all-start = ((bf16[2,96,2048]{1,0,2:T(2,128)(2,1)}), bf16[2,96,2048]{1,0,2:T(2,128)(2,1)S(1)}, u32[]{:S(2)}, u32[]{:S(2)}) async-start(bf16[2,96,2048]{1,0,2:T(2,128)(2,1)} %bitcast.11), calls=%async_computation | async-start | bytes 2097152 | tf_op jit(solution)/shard_map/all_to_all | solution.py:57
  25.1 4.4 %copy.26 = bf16[1,3072,3,128]{1,3,2,0:T(8,128)(2,1)} copy(bf16[1,3072,3,128]{3,1,2,0:T(8,128)(2,1)} %param.11) | data formatting | bytes 4718592 | tf_op args[2]
  30.1 13.1 %all-to-all-done = bf16[2,96,2048]{1,0,2:T(2,128)(2,1)S(1)} async-done(((bf16[2,96,2048]{1,0,2:T(2,128)(2,1)}), bf16[2,96,2048]{1,0,2:T(2,128)(2,1)S(1)}, u32[]{:S(2)}, u32[]{:S(2)}) %all-to-all-start) | async-done | bytes 786464 | tf_op jit(solution)/shard_map/all_to_all | solution.py:57
  43.3 2.7 %fusion.19 = (bf16[1,16,96,128]{2,0,3,1:T(2,128)(2,1)S(1)}, bf16[1,16,96,128]{2,0,3,1:T(2,128)(2,1)}) fusion(bf16[2,16,96,128]{2,0,3,1:T(2,128)(2,1)S(1)} %bitcast.70), kind=kLoop, calls=%fused_computation.33 | loop fusion | bytes 1572864 | tf_op jit(solution)/shard_map/slice | solution.py:63
  46.0 2.3 %copy.30 = bf16[1,16,96,128]{3,2,1,0:T(8,128)(2,1)S(1)} copy(bf16[1,16,96,128]{2,0,3,1:T(2,128)(2,1)} %get-tuple-element.71) | data formatting | bytes 786432 | tf_op jit(solution)/shard_map/slice | solution.py:62
  48.3 1.7 copy.32
  50.1 20.2 %all-gather.3.cloned.1.call-done = bf16[1024,3072]{1,0:T(8,128)(2,1)} async-done(((bf16[64,3072]{1,0:T(8,128)(2,1)}), bf16[1024,3072]{1,0:T(8,128)(2,1)}) %all-gather.3.cloned.1.call-update) | async-done | bytes 6291472 | tf_op jit(solution)/shard_map/all_gather | solution.py:51
  70.3 6.2 %convolution_convert_fusion = bf16[1024,384]{0,1:T(8,128)(2,1)S(1)} fusion(bf16[1024,3072]{1,0:T(8,128)(2,1)} %all-gather.3.cloned.1.call-done, bf16[3072,384]{0,1:T(8,128)(2,1)} %bitcast.72), kind=kOutput, calls=%fused_computation.11 | convolution fusion | flops 2416312320 | bytes 9437184 | tf_op jit(solution)/shard_map/dot_general | solution.py:50
  77.0 0.9 maximum_bitcast_fusion
  78.0 5.8 %while.17 = (s32[]{:T(128)}, bf16[2,512,128]{2,1,0:T(8,128)(2,1)S(1)}, pred[2560]{0:T(1024)(128)(4,1)S(1)}, bf16[2,512,128]{2,1,0:T(8,128)(2,1)S(1)}, bf16[2560,...) while((s32[]{:T(128)}, bf16[2,512,128]{2,1,0:T(8,128)(2,1)S(1)}, ...), condition=%wide.region_5.6_spmd, body=%wide.region_2.5_spmd.sunk | while | flops 681638912 | bytes 19936368 | solution.py:37
  78.0 1.0 fusion.34
  79.8 1.0 fusion.36
  80.9 1.0 fusion.34
  81.8 0.8 fusion.35
  82.7 1.0 fusion.36
  84.5 50.3 %all-gather.5.cloned.1.call-done = bf16[1024,2048]{1,0:T(8,128)(2,1)} async-done(((bf16[1024,128]{1,0:T(8,128)(2,1)}), bf16[1024,2048]{1,0:T(8,128)(2,1)}) %all-gather.5.cloned.1.call-update) | async-done | bytes 4194320 | tf_op jit(solution)/shard_map/all_gather | solution.py:67
  134.8 3.7 %convolution_convert_fusion.1 = bf16[1024,192]{0,1:T(8,128)(2,1)S(1)} fusion(bf16[1024,2048]{1,0:T(8,128)(2,1)} %all-gather.5.cloned.1.call-done, bf16[1,2048,192]{1,2,0:T(8,128)(2,1)S(1)} %copy-done), kind=kOutput, calls=%fused_computation.12 | convolution fusion | flops 805502976 | bytes 5373952 | tf_op jit(solution)/shard_map/dot_general | solution.py:66
  138.7 15.4 %all_to_all.28 = bf16[16,64,192]{2,1,0:T(8,128)(2,1)S(1)} all-to-all(bf16[16,64,192]{2,1,0:T(8,128)(2,1)S(1)} %bitcast.73), channel_id=1, replica_groups=mesh['pipe'=32,'seq'=16] {'seq'}, dimensions={0} | all-to-all | bytes 786432 | tf_op jit(solution)/shard_map/all_to_all | solution.py:71
  155.4 2.0 %collective-permute-start = (bf16[64,3072]{1,0:T(8,128)(2,1)S(1)}, bf16[64,3072]{1,0:T(8,128)(2,1)S(1)}, u32[]{:S(2)}, u32[]{:S(2)}) collective-permute-start(bf16[64,3072]{1,0:T(8,128)(2,1)S(1)} %fusion.16), channel_id=1, source_target_pairs={{0,16},{16,32},{32,48},{48,64},{64,80},{80,96},{96,112},{112,128},... | collective-permute-start | bytes 1179656 | tf_op jit(solution)/shard_map/ppermute | solution.py:12
  157.4 23.5 %collective-permute-done = bf16[64,3072]{1,0:T(8,128)(2,1)S(1)} collective-permute-done((bf16[64,3072]{1,0:T(8,128)(2,1)S(1)}, bf16[64,3072]{1,0:T(8,128)(2,1)S(1)}, u32[]{:S(2)}, u32[]{:S(2)}) %collective-permute-start) | collective-permute-done | bytes 393248 | tf_op jit(solution)/shard_map/ppermute | solution.py:12
  (35 shorter events, 5.2 us)
Async XLA Ops:
  6.5 128.2 %copy-start = (bf16[1,2048,192]{1,2,0:T(8,128)(2,1)S(1)}, bf16[1,2048,192]{1,2,0:T(8,128)(2,1)}, u32[]{:S(2)}) copy-start(bf16[1,2048,192]{1,2,0:T(8,128)(2,1)} %param.12) | copy-start | bytes 2359300
  6.5 63.7 %all-gather.3.cloned.1.call-start = ((), (), s32[]{:S(2)}) async-start(), calls=%async_computation.2 | async-start | bytes 6684672 | tf_op jit(solution)/shard_map/all_gather | solution.py:51
  7.4 22.7 %copy-start.5 = (s32[1536]{0:T(1024)S(1)}, s32[1536]{0:T(1024)}, u32[]{:S(2)}) copy-start(s32[1536]{0:T(1024)} %param.15) | copy-start | bytes 18436
  15.4 27.8 %all-to-all-start = ((bf16[2,96,2048]{1,0,2:T(2,128)(2,1)}), bf16[2,96,2048]{1,0,2:T(2,128)(2,1)S(1)}, u32[]{:S(2)}, u32[]{:S(2)}) async-start(bf16[2,96,2048]{1,0,2:T(2,128)(2,1)} %bitcast.11), calls=%async_computation | async-start | bytes 2097152 | tf_op jit(solution)/shard_map/all_to_all | solution.py:57
  25.0 109.7 %all-gather.5.cloned.1.call-start = ((), (), s32[]{:S(2)}) async-start(), calls=%async_computation.3 | async-start | bytes 4456448 | tf_op jit(solution)/shard_map/all_gather | solution.py:67
  70.3 6.8 %copy-start.2 = (bf16[1,16,96,128]{3,2,1,0:T(8,128)(2,1)S(1)}, bf16[1,16,96,128]{3,2,1,0:T(8,128)(2,1)}, u32[]{:S(2)}) copy-start(bf16[1,16,96,128]{3,2,1,0:T(8,128)(2,1)} %copy.32) | copy-start | bytes 1179652
  78.0 1.8 copy-start.3
  80.8 1.8 copy-start.3
  83.7 0.7 copy-start.4
  138.5 16.8 %copy-start.1 = (bf16[1,64,3072]{2,1,0:T(8,128)(2,1)S(1)}, bf16[1,64,3072]{2,1,0:T(8,128)(2,1)}, u32[]{:S(2)}) copy-start(bf16[1,64,3072]{2,1,0:T(8,128)(2,1)} %param.9) | copy-start | bytes 1179652
  155.4 25.5 %collective-permute-start = (bf16[64,3072]{1,0:T(8,128)(2,1)S(1)}, bf16[64,3072]{1,0:T(8,128)(2,1)S(1)}, u32[]{:S(2)}, u32[]{:S(2)}) collective-permute-start(bf16[64,3072]{1,0:T(8,128)(2,1)S(1)} %fusion.16), channel_id=1, source_target_pairs={{0,16},{16,32},{32,48},{48,64},{64,80},{80,96},{96,112},{112,128},... | collective-permute-start | bytes 1179656 | tf_op jit(solution)/shard_map/ppermute | solution.py:12
Sparse Core Ops, SparseCore 0:
  11.9 58.2 all-gather.2
  84.6 50.1 all-gather.4
where the time goes:
time: 189 us; the launch traced here: 188 us
  waiting for transfers between devices  107 us (57%)
  local copies, waits for them, and re-layouts  18 us (10%)
  blocking collectives  15.4 us (8%)
  between operations  14.2 us (8%)
  matrix products  13.9 us (7%)
  starting transfers between devices  11.6 us (6%)
  other arithmetic  8.03 us (4%)
    all_gather x1, waiting for transfers between devices, on_device(): lax.all_gather(heads_out, 'seq', axis=1, tiled=True)  50.3 us
    ppermute x1, waiting for transfers between devices, from_behind(): return lax.ppermute(value, axis, pairs)  23.5 us
    all_gather x1, waiting for transfers between devices, on_device(): lax.all_gather(hidden, 'seq', axis=0, tiled=True)  20.2 us
    all_to_all x1, blocking collectives, on_device(): lax.all_to_all(projected.astype(jnp.bfloat16), 'seq', split_axis=0, conca...  15.4 us
    all_to_all x1, waiting for transfers between devices, on_device(): lax.all_to_all(stale_kv[0], 'seq', split_axis=2, concat_axis=1, tiled=True)  13.1 us
    unnamed x15, local copies, waits for them, and re-layouts  9.81 us
    all_to_all x1, starting transfers between devices, on_device(): lax.all_to_all(stale_kv[0], 'seq', split_axis=2, concat_axis=1, tiled=True)  9.58 us
    dot_general x1, matrix products, on_device(): jnp.dot(lax.all_gather(hidden, 'seq', axis=0, tiled=True), weight_in, pre...  6.16 us
  transfers between devices with their start and end apart: 4, of which 4 were waited for; matrix products, arithmetic and copies ran while one was open for 8% of the time, Pallas kernels for 0%

commit v1 on v0

v1 whole, which is shorter than its diff:
```python
import jax
import jax.numpy as jnp
from jax import lax
from jax.experimental import pallas as pl
from jax.experimental.pallas import tpu as pltpu
from jax.sharding import PartitionSpec as P

HD = 128
NX, NY, NC = 4, 2, 2
MIB = 1024 * 1024


def microseconds(time):
    return pl.CostEstimate(flops=int(time * 1e9), bytes_accessed=1, transcendentals=0)


X_GROUPS = [[x * NY * NC + rest for x in range(NX)] for rest in range(NY * NC)]


def seq_index(x, y, core):
    return (x % NX) * NY * NC + (y % NY) * NC + core % NC


def shift(value, dx=0, dy=0, dc=0):
    pairs = [
        (seq_index(x, y, c), seq_index(x + dx, y + dy, c + dc))
        for x in range(NX)
        for y in range(NY)
        for c in range(NC)
    ]
    return lax.ppermute(value, "seq", pairs)


def along_x(rows):
    sent = jnp.broadcast_to(rows[None], (NX, *rows.shape))
    return lax.all_to_all(sent, "seq", 0, 0, tiled=True, axis_index_groups=X_GROUPS)


def hand_on(value, dx):
    count = lax.axis_size("pipe")
    pairs = [
        (s * 16 + seq_index(x, y, c), ((s + 1) % count) * 16 + seq_index(x + dx, y, c))
        for s in range(count)
        for x in range(NX)
        for y in range(NY)
        for c in range(NC)
    ]
    return lax.ppermute(value, ("pipe", "seq"), pairs)


def following(first, *values):
    return lax.optimization_barrier((first, *values))[1:]


def whole(count):
    return [pl.BlockSpec(memory_space=pltpu.VMEM)] * count


SCALAR = pl.BlockSpec(memory_space=pltpu.SMEM)


def place(me_ref):
    me = me_ref[0]
    return me >> 2, (me >> 1) & 1, me & 1


def qkv_kernel(rows, mod, w_own, w_sib, own, sib, hidden):
    shift_row = mod[0:1, :]
    scale_row = 1.0 + mod[1:2, :]
    for i in range(NX):
        values = rows[i].astype(jnp.float32)
        mean = jnp.mean(values, axis=-1, keepdims=True)
        centred = values - mean
        var = jnp.mean(centred * centred, axis=-1, keepdims=True)
        normed = centred * lax.rsqrt(var + 1e-06)
        hidden[64 * i : 64 * i + 64, :] = (normed * scale_row + shift_row).astype(jnp.bfloat16)
    parts = [w_own.at[i] for i in range(3)] + [w_sib.at[i] for i in range(3)]
    for pair in range(3):
        weight = jnp.concatenate([parts[2 * pair][...], parts[2 * pair + 1][...]], axis=-1)
        out = jnp.dot(hidden[...], weight, preferred_element_type=jnp.float32).astype(jnp.bfloat16)
        for half in range(2):
            at = 2 * pair + half
            target = own if at < 3 else sib
            target[:, 128 * (at % 3) : 128 * (at % 3) + 128] = out[:, 128 * half : 128 * half + 128]


def project_qkv(rows, mod, w_own, w_sib):
    shape = jax.ShapeDtypeStruct((256, 3 * HD), jnp.bfloat16)
    return pl.pallas_call(
        qkv_kernel,
        out_shape=(shape, shape),
        in_specs=whole(4),
        out_specs=tuple(whole(2)),
        scratch_shapes=[pltpu.VMEM((256, 3072), jnp.bfloat16)],
        compiler_params=pltpu.CompilerParams(vmem_limit_bytes=16 * MIB),
        cost_estimate=microseconds(4.5),
    )(rows, mod, w_own, w_sib)


def attend_kernel(me_ref, micro, patch, p1, s1, p2, s2, stale, out, query, keys, values):
    x, y, c = place(me_ref)
    for i, ref in enumerate((p1, s1, p2, s2)):
        query[i] = ref[:, 0:128]
        keys[256 * i : 256 * i + 256, :] = ref[:, 128:256]
        values[256 * i : 256 * i + 256, :] = ref[:, 256:384]
    for j in range(16):
        keys[1024 + 96 * j : 1120 + 96 * j, :] = stale[j, 0]
        values[1024 + 96 * j : 1120 + 96 * j, :] = stale[j, 1]
    hide = jnp.where(patch[...] != micro[0], 0.0, -jnp.inf)
    for i, (dy, dc) in enumerate(((0, 0), (0, 1), (1, 0), (1, 1))):
        scores = lax.dot_general(
            query[i], keys[...], (((1,), (1,)), ((), ())), preferred_element_type=jnp.float32
        ) * HD ** (-0.5)
        fresh = scores[:, :1024]
        old = scores[:, 1024:] + hide
        top = jnp.maximum(
            jnp.max(fresh, axis=-1, keepdims=True), jnp.max(old, axis=-1, keepdims=True)
        )
        fresh = jnp.exp(fresh - top)
        old = jnp.exp(old - top)
        total = jnp.sum(fresh, axis=-1, keepdims=True) + jnp.sum(old, axis=-1, keepdims=True)
        part = 1.0 / total
        weights = jnp.concatenate(
            [(fresh * part).astype(jnp.bfloat16), (old * part).astype(jnp.bfloat16)], axis=-1
        )
        result = jnp.dot(weights, values[...], preferred_element_type=jnp.float32).astype(jnp.bfloat16)
        group = (y ^ dy) * 2 + (c ^ dc)
        for owner in range(NX):
            for to in range(NX):
                out[to, group, (owner - to) % NX] = result[64 * owner : 64 * owner + 64]


def attend(me, micro, patch, parts, stale):
    return pl.pallas_call(
        attend_kernel,
        out_shape=jax.ShapeDtypeStruct((NX, 4, NX, 64, HD), jnp.bfloat16),
        in_specs=[SCALAR, SCALAR] + whole(6),
        out_specs=whole(1)[0],
        scratch_shapes=[
            pltpu.VMEM((4, 256, HD), jnp.bfloat16),
            pltpu.VMEM((2560, HD), jnp.bfloat16),
            pltpu.VMEM((2560, HD), jnp.bfloat16),
        ],
        compiler_params=pltpu.CompilerParams(vmem_limit_bytes=16 * MIB),
        cost_estimate=microseconds(7),
    )(me, micro, patch, *parts, stale)


def out_kernel(me_ref, heads, w_own, w_c, w_y, w_yc, mod, held, o0, o1, o2, o3, weight):
    x, y, c = place(me_ref)
    for ref, dy, dc in ((w_own, 0, 0), (w_c, 0, 1), (w_y, 1, 0), (w_yc, 1, 1)):
        at = pl.multiple_of(((y ^ dy) * 2 + (c ^ dc)) * 192, 64)
        weight[pl.ds(at, 192), :] = ref[...]
    rows = jnp.concatenate([heads[j] for j in range(16)], axis=-1)
    attn = lax.dot_general(
        rows, weight[...], (((1,), (1,)), ((), ())), preferred_element_type=jnp.float32
    ).astype(jnp.bfloat16).astype(jnp.float32)
    columns = pl.ds(pl.multiple_of(x * 768, 768), 768)
    gate = mod[2:3, columns]
    for i, out in enumerate((o0, o1, o2, o3)):
        values = held[(x + i) & 3, :, columns].astype(jnp.float32)
        out[...] = (values + gate * attn[64 * i : 64 * i + 64, :]).astype(jnp.bfloat16)


def project_out(me, heads, weights, mod, rows):
    shape = jax.ShapeDtypeStruct((64, 768), jnp.bfloat16)
    return pl.pallas_call(
        out_kernel,
        out_shape=(shape,) * 4,
        in_specs=[SCALAR] + whole(7),
        out_specs=tuple(whole(4)),
        scratch_shapes=[pltpu.VMEM((768, 2048), jnp.bfloat16)],
        compiler_params=pltpu.CompilerParams(vmem_limit_bytes=16 * MIB),
        cost_estimate=microseconds(1.5),
    )(me, heads, *weights, mod, rows)


def join_kernel(me_ref, p0, p1, p2, p3, out):
    x, _, _ = place(me_ref)
    for i, ref in enumerate((p0, p1, p2, p3)):
        out[:, pl.ds(pl.multiple_of(((x + NX - i) & 3) * 768, 768), 768)] = ref[...]


def join(me, pieces):
    return pl.pallas_call(
        join_kernel,
        out_shape=jax.ShapeDtypeStruct((64, 3072), jnp.bfloat16),
        in_specs=[SCALAR] + whole(4),
        out_specs=whole(1)[0],
        cost_estimate=microseconds(1.5),
    )(me, *pieces)


def on_device(activations, modulation, w_qkv, w_out, stale_kv, section_micro, patch_micro):
    rows = activations[0]
    mod = modulation[0]
    me = lax.axis_index("seq").astype(jnp.int32).reshape(1)
    w_own = jnp.transpose(w_qkv[0], (1, 0, 2))
    out_own = jnp.transpose(w_out[0], (1, 0))

    across = shift(rows, dy=1)
    near = along_x(rows)
    w_sib = shift(w_own, dc=1)
    there = along_x(across)
    (out_late,) = following(across, out_own)
    out_y = shift(out_late, dy=1)

    own_1, theirs = project_qkv(near, mod, w_own, w_sib)
    sib_1 = shift(theirs, dc=1)
    stale, out_late = following(own_1, stale_kv[0], out_own)
    out_c = shift(out_late, dc=1)
    stale = stale.reshape(2, 96, 16, HD).transpose(2, 0, 1, 3)
    stale = lax.all_to_all(stale, "seq", 0, 0, tiled=True)
    own_2, theirs = project_qkv(there, mod, w_own, w_sib)
    sib_2 = shift(theirs, dc=1)
    out_yc = shift(out_y, dc=1)
    own_2, out_yc = lax.optimization_barrier((own_2, out_yc))

    heads = attend(me, section_micro, patch_micro.reshape(1, -1), (own_1, sib_1, own_2, sib_2), stale)
    heads = lax.all_to_all(heads.reshape(16, 256, HD), "seq", 0, 0, tiled=True)
    pieces = project_out(me, heads, (out_own, out_c, out_y, out_yc), mod, near)
    pieces = [hand_on(piece, dx) for dx, piece in enumerate(pieces)]
    return join(me, pieces)[None]


def solution(mesh):
    return jax.shard_map(
        on_device,
        mesh=mesh,
        in_specs=(
            P("pipe", "seq", None),
            P("pipe", None, None),
            P("pipe", None, None, "seq"),
            P("pipe", None, "seq"),
            P("pipe", None, "seq", None),
            P("pipe"),
            P(),
        ),
        out_specs=P("pipe", "seq", None),
        check_vma=False,
    )
```

time: 189 us -> 150 us (0.79)
  the two profiles are of different devices: /device:TPU:9 before, /device:TPU:6 now
where the time goes in v1:
time: 150 us; the launch traced here: 148 us
  starting transfers between devices  56.4 us (38%)
  waiting for transfers between devices  54 us (36%)
  Pallas kernels  19.9 us (13%)
  local copies, waits for them, and re-layouts  17.2 us (11%)
    all_to_all x2, waiting for transfers between devices, along_x(): lax.all_to_all(sent, 'seq', 0, 0, tiled=True, axis_index_groups=X_GROUPS)  16.1 us
    all_to_all x2, starting transfers between devices, along_x(): lax.all_to_all(sent, 'seq', 0, 0, tiled=True, axis_index_groups=X_GROUPS)  16 us
    ppermute x4, waiting for transfers between devices, hand_on(): return lax.ppermute(value, ('pipe', 'seq'), pairs)  14.7 us
    ppermute x7, starting transfers between devices, shift(): return lax.ppermute(value, 'seq', pairs)  14.3 us
    ppermute x7, waiting for transfers between devices, shift(): return lax.ppermute(value, 'seq', pairs)  14.2 us
    ppermute x4, starting transfers between devices, hand_on(): return lax.ppermute(value, ('pipe', 'seq'), pairs)  14 us
    unnamed x43, local copies, waits for them, and re-layouts  12.5 us
    all_to_all x1, waiting for transfers between devices, on_device(): heads = lax.all_to_all(heads.reshape(16, 256, HD), 'seq', 0, 0, tiled=True)  8.99 us
  transfers between devices with their start and end apart: 15, of which 9 were waited for; matrix products, arithmetic and copies ran while one was open for 3% of the time, Pallas kernels for 6%

profile of v1, /device:TPU:6, one launch (start us, length us, event | category | flops | bytes accessed | tf_op | source)
XLA Modules:
  0.0 148.4 jit_solution(3630452874043122881)
XLA Ops:
  0.0 2.0 %collective-permute-start = (bf16[3,3072,128]{2,1,0:T(8,128)(2,1)}, bf16[3,3072,128]{2,1,0:T(8,128)(2,1)}, u32[]{:S(2)}, u32[]{:S(2)}) collective-permute-start(bf16[3,3072,128]{2,1,0:T(8,128)(2,1)} %bitcast.29), channel_id=1, source_target_pairs={{0,1},{1,0},{2,3},{3,2},{4,5},{5,4},{6,7},{7,6},{8,9},{9,8},{10,11... | collective-permute-start | bytes 7077896 | tf_op jit(solution)/shard_map/ppermute | solution.py:31
  2.1 2.3 %broadcast_in_dim.17 = bf16[4,64,3072]{2,1,0:T(8,128)(2,1)} broadcast(bf16[64,3072]{1,0:T(8,128)(2,1)} %bitcast.32), dimensions={1,2} | broadcast | bytes 1966080 | tf_op jit(solution)/shard_map/broadcast_in_dim | solution.py:35
  4.4 9.5 %all-to-all-start = ((bf16[4,64,3072]{2,1,0:T(8,128)(2,1)}), bf16[4,64,3072]{2,1,0:T(8,128)(2,1)S(1)}, u32[]{:S(2)}, u32[]{:S(2)}) async-start(bf16[4,64,3072]{2,1,0:T(8,128)(2,1)} %broadcast_in_dim.17), calls=%async_computation | async-start | bytes 3145728 | tf_op jit(solution)/shard_map/all_to_all | solution.py:36
  15.8 11.2 %collective-permute-done.2 = bf16[64,3072]{1,0:T(8,128)(2,1)S(1)} collective-permute-done((bf16[64,3072]{1,0:T(8,128)(2,1)S(1)}, bf16[64,3072]{1,0:T(8,128)(2,1)S(1)}, u32[]{:S(2)}, u32[]{:S(2)}) %collective-permute-start.2) | collective-permute-done | bytes 393248 | tf_op jit(solution)/shard_map/ppermute | solution.py:31
  27.0 6.5 %all-to-all-done.rows.held = bf16[4,64,3072]{2,1,0:T(8,128)(2,1)S(1)} async-done(((bf16[4,64,3072]{2,1,0:T(8,128)(2,1)}), bf16[4,64,3072]{2,1,0:T(8,128)(2,1)S(1)}, u32[]{:S(2)}, u32[]{:S(2)}) %all-to-all-start) | async-done | bytes 1572896 | tf_op jit(solution)/shard_map/all_to_all | solution.py:36
  34.9 6.5 %all-to-all-start.1 = ((bf16[4,64,3072]{2,1,0:T(8,128)(2,1)}), bf16[4,64,3072]{2,1,0:T(8,128)(2,1)}, u32[]{:S(2)}, u32[]{:S(2)}) async-start(bf16[4,64,3072]{2,1,0:T(8,128)(2,1)} %broadcast_in_dim.18), calls=%async_computation.1 | async-start | bytes 3145728 | tf_op jit(solution)/shard_map/all_to_all | solution.py:36
  45.0 3.8 %shard_map.73 = (bf16[256,384]{1,0:T(8,128)(2,1)S(1)}, bf16[256,384]{1,0:T(8,128)(2,1)S(1)}) custom-call(bf16[4,64,3072]{2,1,0:T(8,128)(2,1)S(1)} %all-to-all-done.rows.held, f32[3,3072]{1,0:T(4,128)S(1)} %bitcast.26, bf16[3,3072,128]{2,1,0:T(8,128)(2,1)S(1)} %bitcast.30, bf16[3,3072,128]{2,1,0:T(8,128)(2,1)} %collective-permute-done.w_sib), custom_call_target="tpu_custom_call" | custom-call | flops 4499999744 | bytes 1 | tf_op jit(solution)/shard_map/pallas_call | solution.py:89
  50.6 9.7 %all-to-all-done.1.rows = bf16[4,64,3072]{2,1,0:T(8,128)(2,1)} async-done(((bf16[4,64,3072]{2,1,0:T(8,128)(2,1)}), bf16[4,64,3072]{2,1,0:T(8,128)(2,1)}, u32[]{:S(2)}, u32[]{:S(2)}) %all-to-all-start.1) | async-done | bytes 1572896 | tf_op jit(solution)/shard_map/all_to_all | solution.py:36
  60.3 6.3 %all-to-all-start.2 = ((bf16[16,2,96,128]{3,2,1,0:T(8,128)(2,1)}), bf16[16,2,96,128]{3,2,1,0:T(8,128)(2,1)}, u32[]{:S(2)}, u32[]{:S(2)}) async-start(bf16[16,2,96,128]{3,2,1,0:T(8,128)(2,1)} %bitcast_bitcast_fusion), calls=%async_computation.2 | async-start | bytes 1572864 | tf_op jit(solution)/shard_map/all_to_all | solution.py:213
  66.6 2.1 %collective-permute-start.4 = (bf16[192,2048]{1,0:T(8,128)(2,1)}, bf16[192,2048]{1,0:T(8,128)(2,1)S(1)}, u32[]{:S(2)}, u32[]{:S(2)}) collective-permute-start(bf16[192,2048]{1,0:T(8,128)(2,1)} %collective-permute-done.3.w_y), channel_id=1, source_target_pairs={{0,1},{1,0},{2,3},{3,2},{4,5},{5,4},{6,7},{7,6},{8,9},{9,8},{10,11... | collective-permute-start | bytes 2359304 | tf_op jit(solution)/shard_map/ppermute | solution.py:31
  70.3 5.0 %shard_map.74 = (bf16[256,384]{1,0:T(8,128)(2,1)S(1)}, bf16[256,384]{1,0:T(8,128)(2,1)}) custom-call(bf16[4,64,3072]{2,1,0:T(8,128)(2,1)} %all-to-all-done.1.rows, f32[3,3072]{1,0:T(4,128)S(1)} %bitcast.27, bf16[3,3072,128]{2,1,0:T(8,128)(2,1)S(1)} %bitcast.31, bf16[3,3072,128]{2,1,0:T(8,128)(2,1)} %collective-permute-done.w_sib), custom_call_target="tpu_custom_call" | custom-call | flops 4499999744 | bytes 1 | tf_op jit(solution)/shard_map/pallas_call | solution.py:89
  76.0 2.2 %collective-permute-start.5 = (bf16[256,384]{1,0:T(8,128)(2,1)}, bf16[256,384]{1,0:T(8,128)(2,1)}, u32[]{:S(2)}, u32[]{:S(2)}) collective-permute-start(bf16[256,384]{1,0:T(8,128)(2,1)} %get-tuple-element.23), channel_id=1, source_target_pairs={{0,1},{1,0},{2,3},{3,2},{4,5},{5,4},{6,7},{7,6},{8,9},{9,8},{10,11... | collective-permute-start | bytes 589832 | tf_op jit(solution)/shard_map/ppermute | solution.py:31
  78.3 2.1 %collective-permute-start.1 = (bf16[256,384]{1,0:T(8,128)(2,1)S(1)}, bf16[256,384]{1,0:T(8,128)(2,1)}, u32[]{:S(2)}, u32[]{:S(2)}) collective-permute-start(bf16[256,384]{1,0:T(8,128)(2,1)S(1)} %get-tuple-element.19), channel_id=1, source_target_pairs={{0,1},{1,0},{2,3},{3,2},{4,5},{5,4},{6,7},{7,6},{8,9},{9,8},{10,11... | collective-permute-start | bytes 589832 | tf_op jit(solution)/shard_map/ppermute | solution.py:31
  83.6 6.9 %shard_map.75 = bf16[4,4,4,64,128]{4,3,2,1,0:T(8,128)(2,1)S(1)} custom-call(s32[1]{0:T(128)} %bitcast.me_ref, s32[1]{0:T(128)S(6)} %copy.14.micro, s32[1,1536]{1,0:T(1,128)S(1)} %reshape.14.patch, bf16[256,384]{1,0:T(8,128)(2,1)S(1)} %copy-done.11, bf16[256,384]{1,0:T(8,128)(2,1)} %collective-permute-done.1.s1, bf16[256,384]{1,0:T(8,128)(2,1)S(1)} %copy-done.13, ...), custom_call_target="tpu_custom_call" | custom-call | flops 7000000000 | bytes 1 | tf_op jit(solution)/shard_map/pallas_call | solution.py:134
  91.5 5.7 %all-to-all-start.3 = ((bf16[16,256,128]{2,1,0:T(8,128)(2,1)}), bf16[16,256,128]{2,1,0:T(8,128)(2,1)S(1)}, u32[]{:S(2)}, u32[]{:S(2)}) async-start(bf16[16,256,128]{2,1,0:T(8,128)(2,1)} %bitcast.22), calls=%async_computation.3 | async-start | bytes 2097152 | tf_op jit(solution)/shard_map/all_to_all | solution.py:220
  97.2 2.0 %collective-permute-start.6 = (bf16[192,2048]{1,0:T(8,128)(2,1)}, bf16[192,2048]{1,0:T(8,128)(2,1)S(1)}, u32[]{:S(2)}, u32[]{:S(2)}) collective-permute-start(bf16[192,2048]{1,0:T(8,128)(2,1)} %bitcast.23), channel_id=1, source_target_pairs={{0,1},{1,0},{2,3},{3,2},{4,5},{5,4},{6,7},{7,6},{8,9},{9,8},{10,11... | collective-permute-start | bytes 2359304 | tf_op jit(solution)/shard_map/ppermute | solution.py:31
  99.2 2.3 %collective-permute-done.6.w_c = bf16[192,2048]{1,0:T(8,128)(2,1)S(1)} collective-permute-done((bf16[192,2048]{1,0:T(8,128)(2,1)}, bf16[192,2048]{1,0:T(8,128)(2,1)S(1)}, u32[]{:S(2)}, u32[]{:S(2)}) %collective-permute-start.6) | collective-permute-done | bytes 786464 | tf_op jit(solution)/shard_map/ppermute | solution.py:31
  102.4 9.0 %all-to-all-done.3.heads = bf16[16,256,128]{2,1,0:T(8,128)(2,1)S(1)} async-done(((bf16[16,256,128]{2,1,0:T(8,128)(2,1)}), bf16[16,256,128]{2,1,0:T(8,128)(2,1)S(1)}, u32[]{:S(2)}, u32[]{:S(2)}) %all-to-all-start.3) | async-done | bytes 1048608 | tf_op jit(solution)/shard_map/all_to_all | solution.py:220
  114.8 2.4 %shard_map.76 = (bf16[64,768]{1,0:T(8,128)(2,1)S(1)}, bf16[64,768]{1,0:T(8,128)(2,1)S(1)}, bf16[64,768]{1,0:T(8,128)(2,1)S(1)}, bf16[64,768]{1,0:T(8,128)(2,1)S(1)}) custom-call(s32[1]{0:T(128)} %bitcast.me_ref, bf16[16,256,128]{2,1,0:T(8,128)(2,1)S(1)} %all-to-all-done.3.heads, bf16[192,2048]{1,0:T(8,128)(2,1)S(1)} %bitcast.25, ...), custom_call_target="tpu_custom_call" | custom-call | flops 1500000000 | bytes 1 | tf_op jit(solution)/shard_map/pallas_call | solution.py:167
  119.1 3.3 %collective-permute-start.8 = (bf16[64,768]{1,0:T(8,128)(2,1)S(1)}, bf16[64,768]{1,0:T(8,128)(2,1)S(1)}, u32[]{:S(2)}, u32[]{:S(2)}) collective-permute-start(bf16[64,768]{1,0:T(8,128)(2,1)S(1)} %get-tuple-element.28), channel_id=1, source_target_pairs={{0,20},{1,21},{2,22},{3,23},{4,24},{5,25},{6,26},{7,27},{8,28},{9,... | collective-permute-start | bytes 294920 | tf_op jit(solution)/shard_map/ppermute | solution.py:48
  122.5 4.0 %collective-permute-start.9 = (bf16[64,768]{1,0:T(8,128)(2,1)S(1)}, bf16[64,768]{1,0:T(8,128)(2,1)S(1)}, u32[]{:S(2)}, u32[]{:S(2)}) collective-permute-start(bf16[64,768]{1,0:T(8,128)(2,1)S(1)} %get-tuple-element.29), channel_id=1, source_target_pairs={{0,24},{1,25},{2,26},{3,27},{4,28},{5,29},{6,30},{7,31},{8,16},{9,... | collective-permute-start | bytes 294920 | tf_op jit(solution)/shard_map/ppermute | solution.py:48
  126.4 4.8 %collective-permute-start.10 = (bf16[64,768]{1,0:T(8,128)(2,1)S(1)}, bf16[64,768]{1,0:T(8,128)(2,1)S(1)}, u32[]{:S(2)}, u32[]{:S(2)}) collective-permute-start(bf16[64,768]{1,0:T(8,128)(2,1)S(1)} %get-tuple-element.30), channel_id=1, source_target_pairs={{0,28},{1,29},{2,30},{3,31},{4,16},{5,17},{6,18},{7,19},{8,20},{9,... | collective-permute-start | bytes 294920 | tf_op jit(solution)/shard_map/ppermute | solution.py:48
  132.6 11.1 %collective-permute-done.9.p2 = bf16[64,768]{1,0:T(8,128)(2,1)S(1)} collective-permute-done((bf16[64,768]{1,0:T(8,128)(2,1)S(1)}, bf16[64,768]{1,0:T(8,128)(2,1)S(1)}, u32[]{:S(2)}, u32[]{:S(2)}) %collective-permute-start.9) | collective-permute-done | bytes 98336 | tf_op jit(solution)/shard_map/ppermute | solution.py:48
  143.8 2.2 %collective-permute-done.10.p3 = bf16[64,768]{1,0:T(8,128)(2,1)S(1)} collective-permute-done((bf16[64,768]{1,0:T(8,128)(2,1)S(1)}, bf16[64,768]{1,0:T(8,128)(2,1)S(1)}, u32[]{:S(2)}, u32[]{:S(2)}) %collective-permute-start.10) | collective-permute-done | bytes 98336 | tf_op jit(solution)/shard_map/ppermute | solution.py:48
  (58 shorter events, 24.5 us)
Async XLA Ops:
  0.0 49.5 %copy-start = (bf16[1,2,96,2048]{3,2,1,0:T(8,128)(2,1)S(1)}, bf16[1,2,96,2048]{3,2,1,0:T(8,128)(2,1)}, u32[]{:S(2)}) copy-start(bf16[1,2,96,2048]{3,2,1,0:T(8,128)(2,1)} %param.11) | copy-start | bytes 2359300
  0.0 43.3 %collective-permute-start = (bf16[3,3072,128]{2,1,0:T(8,128)(2,1)}, bf16[3,3072,128]{2,1,0:T(8,128)(2,1)}, u32[]{:S(2)}, u32[]{:S(2)}) collective-permute-start(bf16[3,3072,128]{2,1,0:T(8,128)(2,1)} %bitcast.29), channel_id=1, source_target_pairs={{0,1},{1,0},{2,3},{3,2},{4,5},{5,4},{6,7},{7,6},{8,9},{9,8},{10,11... | collective-permute-start | bytes 7077896 | tf_op jit(solution)/shard_map/ppermute | solution.py:31
  4.4 9.5 %copy-start.14 = (bf16[1,64,3072]{2,1,0:T(8,128)(2,1)S(1)}, bf16[1,64,3072]{2,1,0:T(8,128)(2,1)}, u32[]{:S(2)}) copy-start(bf16[1,64,3072]{2,1,0:T(8,128)(2,1)} %param.7) | copy-start | bytes 1179652
  4.4 29.1 %all-to-all-start = ((bf16[4,64,3072]{2,1,0:T(8,128)(2,1)}), bf16[4,64,3072]{2,1,0:T(8,128)(2,1)S(1)}, u32[]{:S(2)}, u32[]{:S(2)}) async-start(bf16[4,64,3072]{2,1,0:T(8,128)(2,1)} %broadcast_in_dim.17), calls=%async_computation | async-start | bytes 3145728 | tf_op jit(solution)/shard_map/all_to_all | solution.py:36
  13.9 13.1 %collective-permute-start.2 = (bf16[64,3072]{1,0:T(8,128)(2,1)S(1)}, bf16[64,3072]{1,0:T(8,128)(2,1)S(1)}, u32[]{:S(2)}, u32[]{:S(2)}) collective-permute-start(bf16[64,3072]{1,0:T(8,128)(2,1)S(1)} %bitcast.33), channel_id=1, source_target_pairs={{0,2},{1,3},{2,0},{3,1},{4,6},{5,7},{6,4},{7,5},{8,10},{9,11},{10,... | collective-permute-start | bytes 1179656 | tf_op jit(solution)/shard_map/ppermute | solution.py:31
  34.9 6.5 %copy-start.15 = (f32[1,3,3072]{2,0,1:T(1,128)S(1)}, f32[1,3,3072]{2,0,1:T(1,128)}, u32[]{:S(2)}) copy-start(f32[1,3,3072]{2,0,1:T(1,128)} %param.8) | copy-start | bytes 110596
  34.9 6.5 %copy-start.2 = (bf16[1,2048,192]{1,2,0:T(8,128)(2,1)S(1)}, bf16[1,2048,192]{1,2,0:T(8,128)(2,1)}, u32[]{:S(2)}) copy-start(bf16[1,2048,192]{1,2,0:T(8,128)(2,1)} %param.10) | copy-start | bytes 2359300
  34.9 25.4 %all-to-all-start.1 = ((bf16[4,64,3072]{2,1,0:T(8,128)(2,1)}), bf16[4,64,3072]{2,1,0:T(8,128)(2,1)}, u32[]{:S(2)}, u32[]{:S(2)}) async-start(bf16[4,64,3072]{2,1,0:T(8,128)(2,1)} %broadcast_in_dim.18), calls=%async_computation.1 | async-start | bytes 3145728 | tf_op jit(solution)/shard_map/all_to_all | solution.py:36
  41.4 25.2 %collective-permute-start.3 = (bf16[192,2048]{1,0:T(8,128)(2,1)S(1)}, bf16[192,2048]{1,0:T(8,128)(2,1)}, u32[]{:S(2)}, u32[]{:S(2)}) collective-permute-start(bf16[192,2048]{1,0:T(8,128)(2,1)S(1)} %bitcast.24), channel_id=1, source_target_pairs={{0,2},{1,3},{2,0},{3,1},{4,6},{5,7},{6,4},{7,5},{8,10},{9,11},{10,... | collective-permute-start | bytes 2359304 | tf_op jit(solution)/shard_map/ppermute | solution.py:31
  60.3 20.7 %copy-start.16 = (s32[1536]{0:T(1024)S(1)}, s32[1536]{0:T(1024)}, u32[]{:S(2)}) copy-start(s32[1536]{0:T(1024)} %param.13) | copy-start | bytes 18436
  60.3 21.4 %all-to-all-start.2 = ((bf16[16,2,96,128]{3,2,1,0:T(8,128)(2,1)}), bf16[16,2,96,128]{3,2,1,0:T(8,128)(2,1)}, u32[]{:S(2)}, u32[]{:S(2)}) async-start(bf16[16,2,96,128]{3,2,1,0:T(8,128)(2,1)} %bitcast_bitcast_fusion), calls=%async_computation.2 | async-start | bytes 1572864 | tf_op jit(solution)/shard_map/all_to_all | solution.py:213
  66.6 14.4 %collective-permute-start.4 = (bf16[192,2048]{1,0:T(8,128)(2,1)}, bf16[192,2048]{1,0:T(8,128)(2,1)S(1)}, u32[]{:S(2)}, u32[]{:S(2)}) collective-permute-start(bf16[192,2048]{1,0:T(8,128)(2,1)} %collective-permute-done.3.w_y), channel_id=1, source_target_pairs={{0,1},{1,0},{2,3},{3,2},{4,5},{5,4},{6,7},{7,6},{8,9},{9,8},{10,11... | collective-permute-start | bytes 2359304 | tf_op jit(solution)/shard_map/ppermute | solution.py:31
  76.0 5.0 %collective-permute-start.5 = (bf16[256,384]{1,0:T(8,128)(2,1)}, bf16[256,384]{1,0:T(8,128)(2,1)}, u32[]{:S(2)}, u32[]{:S(2)}) collective-permute-start(bf16[256,384]{1,0:T(8,128)(2,1)} %get-tuple-element.23), channel_id=1, source_target_pairs={{0,1},{1,0},{2,3},{3,2},{4,5},{5,4},{6,7},{7,6},{8,9},{9,8},{10,11... | collective-permute-start | bytes 589832 | tf_op jit(solution)/shard_map/ppermute | solution.py:31
  78.3 3.5 %collective-permute-start.1 = (bf16[256,384]{1,0:T(8,128)(2,1)S(1)}, bf16[256,384]{1,0:T(8,128)(2,1)}, u32[]{:S(2)}, u32[]{:S(2)}) collective-permute-start(bf16[256,384]{1,0:T(8,128)(2,1)S(1)} %get-tuple-element.19), channel_id=1, source_target_pairs={{0,1},{1,0},{2,3},{3,2},{4,5},{5,4},{6,7},{7,6},{8,9},{9,8},{10,11... | collective-permute-start | bytes 589832 | tf_op jit(solution)/shard_map/ppermute | solution.py:31
  81.0 9.4 %copy-start.4 = (bf16[192,2048]{1,0:T(8,128)(2,1)}, bf16[192,2048]{1,0:T(8,128)(2,1)S(1)}, u32[]{:S(2)}) copy-start(bf16[192,2048]{1,0:T(8,128)(2,1)S(1)} %collective-permute-done.4.w_yc) | copy-start | bytes 2359300
  91.5 20.0 %all-to-all-start.3 = ((bf16[16,256,128]{2,1,0:T(8,128)(2,1)}), bf16[16,256,128]{2,1,0:T(8,128)(2,1)S(1)}, u32[]{:S(2)}, u32[]{:S(2)}) async-start(bf16[16,256,128]{2,1,0:T(8,128)(2,1)} %bitcast.22), calls=%async_computation.3 | async-start | bytes 2097152 | tf_op jit(solution)/shard_map/all_to_all | solution.py:220
  97.2 4.4 %collective-permute-start.6 = (bf16[192,2048]{1,0:T(8,128)(2,1)}, bf16[192,2048]{1,0:T(8,128)(2,1)S(1)}, u32[]{:S(2)}, u32[]{:S(2)}) collective-permute-start(bf16[192,2048]{1,0:T(8,128)(2,1)} %bitcast.23), channel_id=1, source_target_pairs={{0,1},{1,0},{2,3},{3,2},{4,5},{5,4},{6,7},{7,6},{8,9},{9,8},{10,11... | collective-permute-start | bytes 2359304 | tf_op jit(solution)/shard_map/ppermute | solution.py:31
  117.2 15.4 %collective-permute-start.7 = (bf16[64,768]{1,0:T(8,128)(2,1)S(1)}, bf16[64,768]{1,0:T(8,128)(2,1)S(1)}, u32[]{:S(2)}, u32[]{:S(2)}) collective-permute-start(bf16[64,768]{1,0:T(8,128)(2,1)S(1)} %get-tuple-element.27), channel_id=1, source_target_pairs={{0,16},{1,17},{2,18},{3,19},{4,20},{5,21},{6,22},{7,23},{8,24},{9,... | collective-permute-start | bytes 294920 | tf_op jit(solution)/shard_map/ppermute | solution.py:48
  119.1 13.5 %collective-permute-start.8 = (bf16[64,768]{1,0:T(8,128)(2,1)S(1)}, bf16[64,768]{1,0:T(8,128)(2,1)S(1)}, u32[]{:S(2)}, u32[]{:S(2)}) collective-permute-start(bf16[64,768]{1,0:T(8,128)(2,1)S(1)} %get-tuple-element.28), channel_id=1, source_target_pairs={{0,20},{1,21},{2,22},{3,23},{4,24},{5,25},{6,26},{7,27},{8,28},{9,... | collective-permute-start | bytes 294920 | tf_op jit(solution)/shard_map/ppermute | solution.py:48
  122.5 21.3 %collective-permute-start.9 = (bf16[64,768]{1,0:T(8,128)(2,1)S(1)}, bf16[64,768]{1,0:T(8,128)(2,1)S(1)}, u32[]{:S(2)}, u32[]{:S(2)}) collective-permute-start(bf16[64,768]{1,0:T(8,128)(2,1)S(1)} %get-tuple-element.29), channel_id=1, source_target_pairs={{0,24},{1,25},{2,26},{3,27},{4,28},{5,29},{6,30},{7,31},{8,16},{9,... | collective-permute-start | bytes 294920 | tf_op jit(solution)/shard_map/ppermute | solution.py:48
  126.4 19.5 %collective-permute-start.10 = (bf16[64,768]{1,0:T(8,128)(2,1)S(1)}, bf16[64,768]{1,0:T(8,128)(2,1)S(1)}, u32[]{:S(2)}, u32[]{:S(2)}) collective-permute-start(bf16[64,768]{1,0:T(8,128)(2,1)S(1)} %get-tuple-element.30), channel_id=1, source_target_pairs={{0,28},{1,29},{2,30},{3,31},{4,16},{5,17},{6,18},{7,19},{8,20},{9,... | collective-permute-start | bytes 294920 | tf_op jit(solution)/shard_map/ppermute | solution.py:48
  132.6 13.3 %copy-start.17 = (bf16[64,768]{1,0:T(8,128)(2,1)}, bf16[64,768]{1,0:T(8,128)(2,1)S(1)}, u32[]{:S(2)}) copy-start(bf16[64,768]{1,0:T(8,128)(2,1)S(1)} %collective-permute-done.7.p0) | copy-start | bytes 294916
  132.6 13.3 %copy-start.18 = (bf16[64,768]{1,0:T(8,128)(2,1)}, bf16[64,768]{1,0:T(8,128)(2,1)S(1)}, u32[]{:S(2)}) copy-start(bf16[64,768]{1,0:T(8,128)(2,1)S(1)} %collective-permute-done.8.p1) | copy-start | bytes 294916
  143.8 2.2 %copy-start.19 = (bf16[64,768]{1,0:T(8,128)(2,1)}, bf16[64,768]{1,0:T(8,128)(2,1)S(1)}, u32[]{:S(2)}) copy-start(bf16[64,768]{1,0:T(8,128)(2,1)S(1)} %collective-permute-done.9.p2) | copy-start | bytes 294916
  (12 other events, 12.5 us)

commit v2 on v1

v2 whole, which is shorter than its diff:
```python
import math

import jax
import jax.numpy as jnp
from jax import lax
from jax.experimental import pallas as pl
from jax.experimental.pallas import tpu as pltpu
from jax.sharding import PartitionSpec as P

HD = 128
NX, NY, NC = 4, 2, 2
MIB = 1024 * 1024
SCALAR = pl.BlockSpec(memory_space=pltpu.SMEM)
FAR = pl.BlockSpec(memory_space=pltpu.HBM)
NEAR = pl.BlockSpec(memory_space=pltpu.VMEM)


def seq_index(x, y, core):
    return (x % NX) * NY * NC + (y % NY) * NC + core % NC


LANES = [[seq_index(x, y, c) for x in range(NX) for y in range(NY)] for c in range(NC)]


def shift(value, dx=0, dy=0, dc=0):
    pairs = [
        (seq_index(x, y, c), seq_index(x + dx, y + dy, c + dc))
        for x in range(NX)
        for y in range(NY)
        for c in range(NC)
    ]
    return lax.ppermute(value, "seq", pairs)


def hand_on(value, dx):
    count = lax.axis_size("pipe")
    pairs = [
        (s * 16 + seq_index(x, y, c), ((s + 1) % count) * 16 + seq_index(x + dx, y, c))
        for s in range(count)
        for x in range(NX)
        for y in range(NY)
        for c in range(NC)
    ]
    return lax.ppermute(value, ("pipe", "seq"), pairs)


def following(first, *values):
    return lax.optimization_barrier((first, *values))[1:]


def cost(microseconds):
    return pl.CostEstimate(flops=int(microseconds * 1e9), bytes_accessed=1, transcendentals=0)


def params(mib):
    return pltpu.CompilerParams(vmem_limit_bytes=mib * MIB)


def place(me_ref):
    me = me_ref[0]
    return me >> 2, (me >> 1) & 1, me & 1


def pack_kernel(rows, stale, out, held, old, load_sems, row_sems, stale_sems):
    loads = [
        pltpu.make_async_copy(rows, held, load_sems.at[0]),
        pltpu.make_async_copy(stale, old, load_sems.at[1]),
    ]
    for load in loads:
        load.start()
    copies = []
    loads[0].wait()
    for to in range(8):
        copies.append(pltpu.make_async_copy(held, out.at[to, :, 0:3072], row_sems.at[to]))
        copies[-1].start()
    loads[1].wait()
    for to in range(8):
        for t in range(3):
            copies.append(
                pltpu.make_async_copy(
                    old.at[64 * t : 64 * t + 64, 256 * to : 256 * to + 256],
                    out.at[to, :, 3072 + 256 * t : 3328 + 256 * t],
                    stale_sems.at[3 * to + t],
                )
            )
            copies[-1].start()
    for copy in copies:
        copy.wait()


def pack(rows, stale):
    return pl.pallas_call(
        pack_kernel,
        out_shape=jax.ShapeDtypeStruct((8, 64, 3840), jnp.bfloat16),
        in_specs=[FAR, FAR],
        out_specs=FAR,
        scratch_shapes=[
            pltpu.VMEM((64, 3072), jnp.bfloat16),
            pltpu.VMEM((192, 2048), jnp.bfloat16),
            pltpu.SemaphoreType.DMA((2,)),
            pltpu.SemaphoreType.DMA((8,)),
            pltpu.SemaphoreType.DMA((24,)),
        ],
        compiler_params=params(60),
        cost_estimate=cost(3),
    )(rows, stale)


def weights_kernel(w_own, w_sib, weight, sems):
    copies = []
    for i, ref in enumerate((w_sib, w_own)):
        copies.append(pltpu.make_async_copy(ref, weight.at[pl.ds(3 * i, 3)], sems.at[i]))
        copies[-1].start()
    for copy in copies:
        copy.wait()


def collect_weights(w_own, w_sib):
    return pl.pallas_call(
        weights_kernel,
        out_shape=jax.ShapeDtypeStruct((6, 3072, HD), jnp.bfloat16),
        in_specs=[FAR, FAR],
        out_specs=NEAR,
        scratch_shapes=[pltpu.SemaphoreType.DMA((2,))],
        compiler_params=params(16),
        cost_estimate=cost(0.01),
    )(w_own, w_sib)


def qkv_kernel(me_ref, gathered, mod, weight, own, own_old, sib, sib_old, hidden):
    _, _, c = place(me_ref)
    shift_row = mod[0:1, :]
    scale_row = 1.0 + mod[1:2, :]
    for out, head in ((sib_old, 1 - c), (own_old, c)):
        for t in range(3):
            at = pl.multiple_of(3072 + 256 * t + 128 * head, 128)
            out[:, :, 128 * t : 128 * t + 128] = gathered[:, :, pl.ds(at, 128)]
    for half in range(2):
        for i in range(4 * half, 4 * half + 4):
            values = gathered[i, :, 0:3072].astype(jnp.float32)
            mean = jnp.mean(values, axis=-1, keepdims=True)
            centred = values - mean
            var = jnp.mean(centred * centred, axis=-1, keepdims=True)
            normed = centred * lax.rsqrt(var + 1e-06)
            hidden[64 * i : 64 * i + 64, :] = (normed * scale_row + shift_row).astype(jnp.bfloat16)
        for pair in range(3):
            both = jnp.concatenate([weight[2 * pair], weight[2 * pair + 1]], axis=-1)
            result = jnp.dot(
                hidden[256 * half : 256 * half + 256, :], both, preferred_element_type=jnp.float32
            ).astype(jnp.bfloat16)
            for n in range(2):
                at = 2 * pair + n
                target = sib if at < 3 else own
                target[4 * half : 4 * half + 4, :, 128 * (at % 3) : 128 * (at % 3) + 128] = result[
                    :, 128 * n : 128 * n + 128
                ].reshape(4, 64, HD)


def project_qkv(me, gathered, mod, weight):
    shape = jax.ShapeDtypeStruct((8, 64, 3 * HD), jnp.bfloat16)
    return pl.pallas_call(
        qkv_kernel,
        out_shape=(shape,) * 4,
        in_specs=[SCALAR, NEAR, NEAR, NEAR],
        out_specs=(NEAR,) * 4,
        scratch_shapes=[pltpu.VMEM((512, 3072), jnp.bfloat16)],
        compiler_params=params(24),
        cost_estimate=cost(0.01),
    )(me, gathered, mod, weight)


def attend_kernel(me_ref, hide, own, own_old, sib, sib_old, out, query, keys, values, staged, out_sems):
    _, _, c = place(me_ref)
    for i, (new, old) in enumerate(((own, own_old), (sib, sib_old))):
        fresh = slice(512 * i, 512 * i + 512)
        query[fresh, :] = new[:, :, 0:128].reshape(512, HD)
        keys[fresh, :] = new[:, :, 128:256].reshape(512, HD)
        values[fresh, 0:128] = new[:, :, 256:384].reshape(512, HD)
        for k in range(8):
            at = 1024 + 96 * (8 * i + k)
            keys[at : at + 64, :] = old[k, :, 0:128]
            keys[at + 64 : at + 96, :] = old[k, 0:32, 128:256]
            values[at : at + 32, 0:128] = old[k, 32:64, 128:256]
            values[at + 32 : at + 96, 0:128] = old[k, :, 256:384]
    values[:, 128:256] = jnp.ones((2560, 128), jnp.bfloat16)
    scale = HD ** (-0.5) * math.log2(math.e)
    for i in range(8):
        scores = lax.dot_general(
            query[128 * i : 128 * i + 128, :],
            keys[...],
            (((1,), (1,)), ((), ())),
            preferred_element_type=jnp.float32,
        )
        fresh = scores[:, :1024]
        old = scores[:, 1024:] + hide[...]
        top = jnp.maximum(
            jnp.max(fresh, axis=-1, keepdims=True), jnp.max(old, axis=-1, keepdims=True)
        )
        weights = jnp.concatenate(
            [
                jnp.exp2((fresh - top) * scale).astype(jnp.bfloat16),
                jnp.exp2((old - top) * scale).astype(jnp.bfloat16),
            ],
            axis=-1,
        )
        summed = jnp.dot(weights, values[...], preferred_element_type=jnp.float32)
        result = (summed[:, :128] * (1.0 / summed[:, 128:])).astype(jnp.bfloat16)
        for n in range(2):
            dc, owner, y = i // 4, i % 4, n
            for to in range(NX):
                staged[to, y * 2 + (c ^ dc), (owner - to) % NX] = result[64 * n : 64 * n + 64]
    stores = []
    for to in range(NX):
        stores.append(pltpu.make_async_copy(staged.at[to], out.at[to], out_sems.at[to]))
        stores[-1].start()
    for store in stores:
        store.wait()


def attend(me, hide, own, own_old, sib, sib_old):
    return pl.pallas_call(
        attend_kernel,
        out_shape=jax.ShapeDtypeStruct((NX, 4, NX, 64, HD), jnp.bfloat16),
        in_specs=[SCALAR] + [NEAR] * 5,
        out_specs=FAR,
        scratch_shapes=[
            pltpu.VMEM((1024, HD), jnp.bfloat16),
            pltpu.VMEM((2560, HD), jnp.bfloat16),
            pltpu.VMEM((2560, 2 * HD), jnp.bfloat16),
            pltpu.VMEM((NX, 4, NX, 64, HD), jnp.bfloat16),
            pltpu.SemaphoreType.DMA((NX,)),
        ],
        compiler_params=params(32),
        cost_estimate=cost(0.01),
    )(me, hide, own, own_old, sib, sib_old)


def out_kernel(me_ref, heads, w_own, w_c, w_y, w_yc, mod, gathered, o0, o1, o2, o3, weight, held, w_sems, sems):
    x, y, c = place(me_ref)
    parts = []
    for i, (ref, dy, dc) in enumerate(((w_own, 0, 0), (w_c, 0, 1), (w_y, 1, 0), (w_yc, 1, 1))):
        at = pl.multiple_of(((y ^ dy) * 2 + (c ^ dc)) * 192, 64)
        parts.append(pltpu.make_async_copy(ref, weight.at[pl.ds(at, 192), :], w_sems.at[i]))
        parts[-1].start()
    columns = pl.ds(pl.multiple_of(x * 768, 768), 768)
    loads = [
        pltpu.make_async_copy(
            gathered.at[((x + i) & 3) * 2 + y, :, columns], held.at[i], sems.at[i]
        )
        for i in range(4)
    ]
    for load in loads:
        load.start()
    rows = jnp.concatenate([heads[j] for j in range(16)], axis=-1)
    for part in parts:
        part.wait()
    attn = lax.dot_general(
        rows, weight[...], (((1,), (1,)), ((), ())), preferred_element_type=jnp.float32
    ).astype(jnp.bfloat16).astype(jnp.float32)
    gate = mod[2:3, columns]
    for i, out in enumerate((o0, o1, o2, o3)):
        loads[i].wait()
        values = held[i].astype(jnp.float32)
        out[...] = (values + gate * attn[64 * i : 64 * i + 64, :]).astype(jnp.bfloat16)


def project_out(me, heads, weights, mod, gathered):
    shape = jax.ShapeDtypeStruct((64, 768), jnp.bfloat16)
    return pl.pallas_call(
        out_kernel,
        out_shape=(shape,) * 4,
        in_specs=[SCALAR, NEAR] + [FAR] * 4 + [NEAR, FAR],
        out_specs=(NEAR,) * 4,
        scratch_shapes=[
            pltpu.VMEM((768, 2048), jnp.bfloat16),
            pltpu.VMEM((4, 64, 768), jnp.bfloat16),
            pltpu.SemaphoreType.DMA((4,)),
            pltpu.SemaphoreType.DMA((4,)),
        ],
        compiler_params=params(32),
        cost_estimate=cost(2),
    )(me, heads, *weights, mod, gathered)


def join_kernel(me_ref, p0, p1, p2, p3, out, sems):
    x, _, _ = place(me_ref)
    copies = []
    for i, ref in enumerate((p0, p1, p2, p3)):
        columns = pl.ds(pl.multiple_of(((x + NX - i) & 3) * 768, 768), 768)
        copies.append(pltpu.make_async_copy(ref, out.at[:, columns], sems.at[i]))
        copies[-1].start()
    for copy in copies:
        copy.wait()


def join(me, pieces):
    return pl.pallas_call(
        join_kernel,
        out_shape=jax.ShapeDtypeStruct((64, 3072), jnp.bfloat16),
        in_specs=[SCALAR] + [NEAR] * 4,
        out_specs=FAR,
        scratch_shapes=[pltpu.SemaphoreType.DMA((4,))],
        compiler_params=params(32),
        cost_estimate=cost(0.01),
    )(me, *pieces)


def on_device(activations, modulation, w_qkv, w_out, stale_kv, section_micro, patch_micro):
    rows = activations[0]
    mod = modulation[0]
    index = lax.axis_index("seq").astype(jnp.int32)
    me = index.reshape(1)
    w_own = jnp.transpose(w_qkv[0], (1, 0, 2))
    out_own = jnp.transpose(w_out[0], (1, 0))
    owners = patch_micro.reshape(8, 2, 96).transpose(1, 0, 2)
    owners = jnp.where(index % 2 == 0, owners, owners[::-1]).reshape(1, -1)
    hide = jnp.where(owners != section_micro[0], 0.0, -jnp.inf).astype(jnp.float32)

    sent = pack(rows, stale_kv[0].reshape(192, 2048))
    gathered = lax.all_to_all(sent, "seq", 0, 0, tiled=True, axis_index_groups=LANES)
    w_sib = shift(w_own, dc=1)
    out_c = shift(out_own, dc=1)
    (out_late,) = following(gathered, out_own)
    out_y = shift(out_late, dy=1)
    out_yc = shift(out_y, dc=1)
    own, own_old, sib, sib_old = project_qkv(me, gathered, mod, collect_weights(w_own, w_sib))
    sib = shift(sib, dc=1)
    sib_old = shift(sib_old, dc=1)
    heads = attend(me, hide, own, own_old, sib, sib_old)
    (heads,) = following(out_y, heads)
    heads = lax.all_to_all(heads.reshape(16, 256, HD), "seq", 0, 0, tiled=True)
    pieces = project_out(me, heads, (out_own, out_c, out_y, out_yc), mod, gathered)
    pieces = [hand_on(piece, dx) for dx, piece in enumerate(pieces)]
    return join(me, pieces)[None]


def solution(mesh):
    return jax.shard_map(
        on_device,
        mesh=mesh,
        in_specs=(
            P("pipe", "seq", None),
            P("pipe", None, None),
            P("pipe", None, None, "seq"),
            P("pipe", None, "seq"),
            P("pipe", None, "seq", None),
            P("pipe"),
            P(),
        ),
        out_specs=P("pipe", "seq", None),
        check_vma=False,
    )
```

time: 150 us -> 134 us (0.89)
  local copies, waits for them, and re-layouts: 17.2 us -> 2.26 us
  starting transfers between devices: 56.4 us -> 47.6 us
  waiting for transfers between devices: 54 us -> 62.8 us
    all_to_all x3 -> x1, waiting for transfers between devices: 16.1 us -> 39.2 us  [on_device(): lax.all_to_all(sent, 'seq', 0, 0, tiled=True, axis_index_groups=LANES)]
    all_to_all x3 -> x1, starting transfers between devices: 22.3 us -> 10.6 us  [on_device(): lax.all_to_all(sent, 'seq', 0, 0, tiled=True, axis_index_groups=LANES)]
    ppermute x7 -> x6, waiting for transfers between devices: 14.2 us -> 2.54 us  [shift(): return lax.ppermute(value, 'seq', pairs)]
    unnamed x43 -> x13, local copies, waits for them, and re-layouts: 12.5 us -> 2.07 us
    ppermute x4, starting transfers between devices: 14 us -> 18.6 us  [hand_on(): return lax.ppermute(value, ('pipe', 'seq'), pairs)]
    broadcast_in_dim x2 -> x0, local copies, waits for them, and re-layouts: 3.69 us -> none  [along_x(): sent = jnp.broadcast_to(rows[None], (NX, *rows.shape))]
    pallas_call x3 -> x4, Pallas kernels: 11.2 us -> 14.2 us  [the longest x1 6.86 us: project_qkv(): pl.pallas_call(qkv_kernel, out_shape=(shape,) * 4, in_specs=[SCALAR, NEAR...]
    all_to_all x1, waiting for transfers between devices: 8.99 us -> 6.91 us  [on_device(): heads = lax.all_to_all(heads.reshape(16, 256, HD), 'seq', 0, 0, tiled=True)]
  transfers between devices with their start and end apart: 15 -> 12, of which waited for: 9 -> 8; matrix products, arithmetic and copies ran while one was open for 3% -> 0% of each run, Pallas kernels for 6% -> 10%
where the time goes in v2:
time: 134 us; the launch traced here: 133 us
  waiting for transfers between devices  62.8 us (47%)
  starting transfers between devices  47.6 us (36%)
  Pallas kernels  19.8 us (15%)
  local copies, waits for them, and re-layouts  2.26 us (2%)
    all_to_all x1, waiting for transfers between devices, on_device(): lax.all_to_all(sent, 'seq', 0, 0, tiled=True, axis_index_groups=LANES)  39.2 us
    ppermute x4, starting transfers between devices, hand_on(): return lax.ppermute(value, ('pipe', 'seq'), pairs)  18.6 us
    ppermute x4, waiting for transfers between devices, hand_on(): return lax.ppermute(value, ('pipe', 'seq'), pairs)  14.1 us
    ppermute x6, starting transfers between devices, shift(): return lax.ppermute(value, 'seq', pairs)  12.4 us
    all_to_all x1, starting transfers between devices, on_device(): lax.all_to_all(sent, 'seq', 0, 0, tiled=True, axis_index_groups=LANES)  10.6 us
    all_to_all x1, waiting for transfers between devices, on_device(): heads = lax.all_to_all(heads.reshape(16, 256, HD), 'seq', 0, 0, tiled=True)  6.91 us
    pallas_call x1, Pallas kernels, project_qkv(): pl.pallas_call(qkv_kernel, out_shape=(shape,) * 4, in_specs=[SCALAR, NEAR...  6.86 us
    all_to_all x1, starting transfers between devices, on_device(): heads = lax.all_to_all(heads.reshape(16, 256, HD), 'seq', 0, 0, tiled=True)  6 us
  transfers between devices with their start and end apart: 12, of which 8 were waited for; matrix products, arithmetic and copies ran while one was open for 0% of the time, Pallas kernels for 10%

profile of v2, /device:TPU:6, one launch (start us, length us, event | category | flops | bytes accessed | tf_op | source)
XLA Modules:
  0.0 133.4 jit_solution(2281050136028007259)
XLA Ops:
  0.0 3.2 %shard_map.73 = bf16[8,64,3840]{2,1,0:T(8,128)(2,1)} custom-call(bf16[64,3072]{1,0:T(8,128)(2,1)} %bitcast.27, bf16[192,2048]{1,0:T(8,128)(2,1)} %bitcast.26), custom_call_target="tpu_custom_call" | custom-call | flops 3000000000 | bytes 1 | tf_op jit(solution)/shard_map/pallas_call | solution.py:92
  3.3 10.6 %all-to-all-start = ((bf16[8,64,3840]{2,1,0:T(8,128)(2,1)}), bf16[8,64,3840]{2,1,0:T(8,128)(2,1)}, u32[]{:S(2)}, u32[]{:S(2)}) async-start(bf16[8,64,3840]{2,1,0:T(8,128)(2,1)} %shard_map.73), calls=%async_computation | async-start | bytes 7864320 | tf_op jit(solution)/shard_map/all_to_all | solution.py:320
  13.8 1.9 %collective-permute-start.1 = (bf16[3,3072,128]{2,1,0:T(8,128)(2,1)S(1)}, bf16[3,3072,128]{2,1,0:T(8,128)(2,1)}, u32[]{:S(2)}, u32[]{:S(2)}) collective-permute-start(bf16[3,3072,128]{2,1,0:T(8,128)(2,1)S(1)} %bitcast.18), channel_id=1, source_target_pairs={{0,1},{1,0},{2,3},{3,2},{4,5},{5,4},{6,7},{7,6},{8,9},{9,8},{10,11... | collective-permute-start | bytes 7077896 | tf_op jit(solution)/shard_map/ppermute | solution.py:32
  15.8 39.2 %all-to-all-done.gathered = bf16[8,64,3840]{2,1,0:T(8,128)(2,1)} async-done(((bf16[8,64,3840]{2,1,0:T(8,128)(2,1)}), bf16[8,64,3840]{2,1,0:T(8,128)(2,1)}, u32[]{:S(2)}, u32[]{:S(2)}) %all-to-all-start) | async-done | bytes 3932192 | tf_op jit(solution)/shard_map/all_to_all | solution.py:320
  55.0 1.9 %collective-permute-start = (bf16[192,2048]{1,0:T(8,128)(2,1)S(1)}, bf16[192,2048]{1,0:T(8,128)(2,1)}, u32[]{:S(2)}, u32[]{:S(2)}) collective-permute-start(bf16[192,2048]{1,0:T(8,128)(2,1)S(1)} %bitcast.20), channel_id=1, source_target_pairs={{0,2},{1,3},{2,0},{3,1},{4,6},{5,7},{6,4},{7,5},{8,10},{9,11},{10,... | collective-permute-start | bytes 2359304 | tf_op jit(solution)/shard_map/ppermute | solution.py:32
  56.9 1.7 %shard_map.74.weight = bf16[6,3072,128]{2,1,0:T(8,128)(2,1)S(1)} custom-call(bf16[3,3072,128]{2,1,0:T(8,128)(2,1)S(1)} %bitcast.19, bf16[3,3072,128]{2,1,0:T(8,128)(2,1)} %collective-permute-done.1.w_sib), custom_call_target="tpu_custom_call" | custom-call | flops 10000000 | bytes 1 | tf_op jit(solution)/shard_map/pallas_call | solution.py:119
  58.6 6.9 %shard_map.75 = (bf16[8,64,384]{2,1,0:T(8,128)(2,1)S(1)}, bf16[8,64,384]{2,1,0:T(8,128)(2,1)S(1)}, bf16[8,64,384]{2,1,0:T(8,128)(2,1)}, bf16[8,64,384]{2,1,0:T(8,128)(2,1)S(1)}) custom-call(s32[1]{0:T(128)} %bitcast.me_ref, bf16[8,64,3840]{2,1,0:T(8,128)(2,1)} %all-to-all-done.gathered, f32[3,3072]{1,0:T(4,128)S(1)} %bitcast.23, ...), custom_call_target="tpu_custom_call" | custom-call | flops 10000000 | bytes 1 | tf_op jit(solution)/shard_map/pallas_call | solution.py:161
  65.5 1.9 %collective-permute-start.2 = (bf16[8,64,384]{2,1,0:T(8,128)(2,1)}, bf16[8,64,384]{2,1,0:T(8,128)(2,1)S(1)}, u32[]{:S(2)}, u32[]{:S(2)}) collective-permute-start(bf16[8,64,384]{2,1,0:T(8,128)(2,1)} %get-tuple-element.18), channel_id=1, source_target_pairs={{0,1},{1,0},{2,3},{3,2},{4,5},{5,4},{6,7},{7,6},{8,9},{9,8},{10,11... | collective-permute-start | bytes 1179656 | tf_op jit(solution)/shard_map/ppermute | solution.py:32
  67.4 2.4 %collective-permute-start.3 = (bf16[8,64,384]{2,1,0:T(8,128)(2,1)S(1)}, bf16[8,64,384]{2,1,0:T(8,128)(2,1)S(1)}, u32[]{:S(2)}, u32[]{:S(2)}) collective-permute-start(bf16[8,64,384]{2,1,0:T(8,128)(2,1)S(1)} %get-tuple-element.19), channel_id=1, source_target_pairs={{0,1},{1,0},{2,3},{3,2},{4,5},{5,4},{6,7},{7,6},{8,9},{9,8},{10,11... | collective-permute-start | bytes 1179656 | tf_op jit(solution)/shard_map/ppermute | solution.py:32
  71.1 4.8 %shard_map.76 = bf16[4,4,4,64,128]{4,3,2,1,0:T(8,128)(2,1)} custom-call(s32[1]{0:T(128)} %bitcast.me_ref, f32[1,1536]{1,0:T(1,128)S(1)} %select_n.25.hide, bf16[8,64,384]{2,1,0:T(8,128)(2,1)S(1)} %get-tuple-element.16.own, bf16[8,64,384]{2,1,0:T(8,128)(2,1)S(1)} %get-tuple-element.17.own_old, bf16[8,64,384]{2,1,0:T(8,128)(2,1)S(1)} %collective-permute-done.2.sib, ...), custom_call_target="tpu_custom_call" | custom-call | flops 10000000 | bytes 1 | tf_op jit(solution)/shard_map/pallas_call | solution.py:221
  76.0 6.0 %all-to-all-start.1 = ((bf16[16,256,128]{2,1,0:T(8,128)(2,1)}), bf16[16,256,128]{2,1,0:T(8,128)(2,1)S(1)}, u32[]{:S(2)}, u32[]{:S(2)}) async-start(bf16[16,256,128]{2,1,0:T(8,128)(2,1)} %bitcast.10), calls=%async_computation.1 | async-start | bytes 2097152 | tf_op jit(solution)/shard_map/all_to_all | solution.py:331
  82.0 2.0 %collective-permute-start.4 = (bf16[192,2048]{1,0:T(8,128)(2,1)S(1)}, bf16[192,2048]{1,0:T(8,128)(2,1)S(1)}, u32[]{:S(2)}, u32[]{:S(2)}) collective-permute-start(bf16[192,2048]{1,0:T(8,128)(2,1)S(1)} %bitcast.21), channel_id=1, source_target_pairs={{0,1},{1,0},{2,3},{3,2},{4,5},{5,4},{6,7},{7,6},{8,9},{9,8},{10,11... | collective-permute-start | bytes 2359304 | tf_op jit(solution)/shard_map/ppermute | solution.py:32
  84.0 2.3 %collective-permute-start.5 = (bf16[192,2048]{1,0:T(8,128)(2,1)}, bf16[192,2048]{1,0:T(8,128)(2,1)S(1)}, u32[]{:S(2)}, u32[]{:S(2)}) collective-permute-start(bf16[192,2048]{1,0:T(8,128)(2,1)} %collective-permute-done.w_y), channel_id=1, source_target_pairs={{0,1},{1,0},{2,3},{3,2},{4,5},{5,4},{6,7},{7,6},{8,9},{9,8},{10,11... | collective-permute-start | bytes 2359304 | tf_op jit(solution)/shard_map/ppermute | solution.py:32
  86.3 2.1 %collective-permute-done.5.w_yc = bf16[192,2048]{1,0:T(8,128)(2,1)S(1)} collective-permute-done((bf16[192,2048]{1,0:T(8,128)(2,1)}, bf16[192,2048]{1,0:T(8,128)(2,1)S(1)}, u32[]{:S(2)}, u32[]{:S(2)}) %collective-permute-start.5) | collective-permute-done | bytes 786464 | tf_op jit(solution)/shard_map/ppermute | solution.py:32
  89.3 6.9 %all-to-all-done.1.heads = bf16[16,256,128]{2,1,0:T(8,128)(2,1)S(1)} async-done(((bf16[16,256,128]{2,1,0:T(8,128)(2,1)}), bf16[16,256,128]{2,1,0:T(8,128)(2,1)S(1)}, u32[]{:S(2)}, u32[]{:S(2)}) %all-to-all-start.1) | async-done | bytes 1048608 | tf_op jit(solution)/shard_map/all_to_all | solution.py:331
  96.2 1.1 copy-done.3
  97.4 2.5 %shard_map.77 = (bf16[64,768]{1,0:T(8,128)(2,1)S(1)}, bf16[64,768]{1,0:T(8,128)(2,1)S(1)}, bf16[64,768]{1,0:T(8,128)(2,1)S(1)}, bf16[64,768]{1,0:T(8,128)(2,1)S(1)}) custom-call(s32[1]{0:T(128)} %bitcast.me_ref, bf16[16,256,128]{2,1,0:T(8,128)(2,1)S(1)} %all-to-all-done.1.heads, bf16[192,2048]{1,0:T(8,128)(2,1)S(1)} %bitcast.22, ...), custom_call_target="tpu_custom_call" | custom-call | flops 2000000000 | bytes 1 | tf_op jit(solution)/shard_map/pallas_call | solution.py:269
  99.8 3.7 %collective-permute-start.6 = (bf16[64,768]{1,0:T(8,128)(2,1)S(1)}, bf16[64,768]{1,0:T(8,128)(2,1)S(1)}, u32[]{:S(2)}, u32[]{:S(2)}) collective-permute-start(bf16[64,768]{1,0:T(8,128)(2,1)S(1)} %get-tuple-element.21), channel_id=1, source_target_pairs={{0,16},{1,17},{2,18},{3,19},{4,20},{5,21},{6,22},{7,23},{8,24},{9,... | collective-permute-start | bytes 294920 | tf_op jit(solution)/shard_map/ppermute | solution.py:44
  103.6 6.2 %collective-permute-start.7 = (bf16[64,768]{1,0:T(8,128)(2,1)S(1)}, bf16[64,768]{1,0:T(8,128)(2,1)S(1)}, u32[]{:S(2)}, u32[]{:S(2)}) collective-permute-start(bf16[64,768]{1,0:T(8,128)(2,1)S(1)} %get-tuple-element.22), channel_id=1, source_target_pairs={{0,20},{1,21},{2,22},{3,23},{4,24},{5,25},{6,26},{7,27},{8,28},{9,... | collective-permute-start | bytes 294920 | tf_op jit(solution)/shard_map/ppermute | solution.py:44
  109.8 3.9 %collective-permute-start.8 = (bf16[64,768]{1,0:T(8,128)(2,1)S(1)}, bf16[64,768]{1,0:T(8,128)(2,1)S(1)}, u32[]{:S(2)}, u32[]{:S(2)}) collective-permute-start(bf16[64,768]{1,0:T(8,128)(2,1)S(1)} %get-tuple-element.23), channel_id=1, source_target_pairs={{0,24},{1,25},{2,26},{3,27},{4,28},{5,29},{6,30},{7,31},{8,16},{9,... | collective-permute-start | bytes 294920 | tf_op jit(solution)/shard_map/ppermute | solution.py:44
  113.7 4.8 %collective-permute-start.9 = (bf16[64,768]{1,0:T(8,128)(2,1)S(1)}, bf16[64,768]{1,0:T(8,128)(2,1)S(1)}, u32[]{:S(2)}, u32[]{:S(2)}) collective-permute-start(bf16[64,768]{1,0:T(8,128)(2,1)S(1)} %get-tuple-element.24), channel_id=1, source_target_pairs={{0,28},{1,29},{2,30},{3,31},{4,16},{5,17},{6,18},{7,19},{8,20},{9,... | collective-permute-start | bytes 294920 | tf_op jit(solution)/shard_map/ppermute | solution.py:44
  118.5 1.0 collective-permute-done.6.p0
  119.8 10.8 %collective-permute-done.8.p2 = bf16[64,768]{1,0:T(8,128)(2,1)S(1)} collective-permute-done((bf16[64,768]{1,0:T(8,128)(2,1)S(1)}, bf16[64,768]{1,0:T(8,128)(2,1)S(1)}, u32[]{:S(2)}, u32[]{:S(2)}) %collective-permute-start.8) | collective-permute-done | bytes 98336 | tf_op jit(solution)/shard_map/ppermute | solution.py:44
  130.7 1.9 %collective-permute-done.9.p3 = bf16[64,768]{1,0:T(8,128)(2,1)S(1)} collective-permute-done((bf16[64,768]{1,0:T(8,128)(2,1)S(1)}, bf16[64,768]{1,0:T(8,128)(2,1)S(1)}, u32[]{:S(2)}, u32[]{:S(2)}) %collective-permute-start.9) | collective-permute-done | bytes 98336 | tf_op jit(solution)/shard_map/ppermute | solution.py:44
  (24 shorter events, 2.7 us)
Async XLA Ops:
  3.2 10.6 %copy-start = (bf16[1,3072,3,128]{3,1,2,0:T(8,128)(2,1)S(1)}, bf16[1,3072,3,128]{3,1,2,0:T(8,128)(2,1)}, u32[]{:S(2)}) copy-start(bf16[1,3072,3,128]{3,1,2,0:T(8,128)(2,1)} %param.9) | copy-start | bytes 7077892
  3.3 51.7 %copy-start.1 = (bf16[1,2048,192]{1,2,0:T(8,128)(2,1)S(1)}, bf16[1,2048,192]{1,2,0:T(8,128)(2,1)}, u32[]{:S(2)}) copy-start(bf16[1,2048,192]{1,2,0:T(8,128)(2,1)} %param.10) | copy-start | bytes 2359300
  3.3 53.6 %copy-start.4 = (f32[1,3,3072]{2,0,1:T(1,128)S(1)}, f32[1,3,3072]{2,0,1:T(1,128)}, u32[]{:S(2)}) copy-start(f32[1,3,3072]{2,0,1:T(1,128)} %param.8) | copy-start | bytes 110596
  3.3 51.7 %all-to-all-start = ((bf16[8,64,3840]{2,1,0:T(8,128)(2,1)}), bf16[8,64,3840]{2,1,0:T(8,128)(2,1)}, u32[]{:S(2)}, u32[]{:S(2)}) async-start(bf16[8,64,3840]{2,1,0:T(8,128)(2,1)} %shard_map.73), calls=%async_computation | async-start | bytes 7864320 | tf_op jit(solution)/shard_map/all_to_all | solution.py:320
  13.8 43.1 %collective-permute-start.1 = (bf16[3,3072,128]{2,1,0:T(8,128)(2,1)S(1)}, bf16[3,3072,128]{2,1,0:T(8,128)(2,1)}, u32[]{:S(2)}, u32[]{:S(2)}) collective-permute-start(bf16[3,3072,128]{2,1,0:T(8,128)(2,1)S(1)} %bitcast.18), channel_id=1, source_target_pairs={{0,1},{1,0},{2,3},{3,2},{4,5},{5,4},{6,7},{7,6},{8,9},{9,8},{10,11... | collective-permute-start | bytes 7077896 | tf_op jit(solution)/shard_map/ppermute | solution.py:32
  55.0 21.0 %collective-permute-start = (bf16[192,2048]{1,0:T(8,128)(2,1)S(1)}, bf16[192,2048]{1,0:T(8,128)(2,1)}, u32[]{:S(2)}, u32[]{:S(2)}) collective-permute-start(bf16[192,2048]{1,0:T(8,128)(2,1)S(1)} %bitcast.20), channel_id=1, source_target_pairs={{0,2},{1,3},{2,0},{3,1},{4,6},{5,7},{6,4},{7,5},{8,10},{9,11},{10,... | collective-permute-start | bytes 2359304 | tf_op jit(solution)/shard_map/ppermute | solution.py:32
  58.6 11.2 %copy-start.5 = (s32[1536]{0:T(1024)S(1)}, s32[1536]{0:T(1024)}, u32[]{:S(2)}) copy-start(s32[1536]{0:T(1024)} %param.13) | copy-start | bytes 18436
  65.5 5.2 %collective-permute-start.2 = (bf16[8,64,384]{2,1,0:T(8,128)(2,1)}, bf16[8,64,384]{2,1,0:T(8,128)(2,1)S(1)}, u32[]{:S(2)}, u32[]{:S(2)}) collective-permute-start(bf16[8,64,384]{2,1,0:T(8,128)(2,1)} %get-tuple-element.18), channel_id=1, source_target_pairs={{0,1},{1,0},{2,3},{3,2},{4,5},{5,4},{6,7},{7,6},{8,9},{9,8},{10,11... | collective-permute-start | bytes 1179656 | tf_op jit(solution)/shard_map/ppermute | solution.py:32
  67.4 3.7 %collective-permute-start.3 = (bf16[8,64,384]{2,1,0:T(8,128)(2,1)S(1)}, bf16[8,64,384]{2,1,0:T(8,128)(2,1)S(1)}, u32[]{:S(2)}, u32[]{:S(2)}) collective-permute-start(bf16[8,64,384]{2,1,0:T(8,128)(2,1)S(1)} %get-tuple-element.19), channel_id=1, source_target_pairs={{0,1},{1,0},{2,3},{3,2},{4,5},{5,4},{6,7},{7,6},{8,9},{9,8},{10,11... | collective-permute-start | bytes 1179656 | tf_op jit(solution)/shard_map/ppermute | solution.py:32
  76.0 20.2 %all-to-all-start.1 = ((bf16[16,256,128]{2,1,0:T(8,128)(2,1)}), bf16[16,256,128]{2,1,0:T(8,128)(2,1)S(1)}, u32[]{:S(2)}, u32[]{:S(2)}) async-start(bf16[16,256,128]{2,1,0:T(8,128)(2,1)} %bitcast.10), calls=%async_computation.1 | async-start | bytes 2097152 | tf_op jit(solution)/shard_map/all_to_all | solution.py:331
  82.0 4.3 %collective-permute-start.4 = (bf16[192,2048]{1,0:T(8,128)(2,1)S(1)}, bf16[192,2048]{1,0:T(8,128)(2,1)S(1)}, u32[]{:S(2)}, u32[]{:S(2)}) collective-permute-start(bf16[192,2048]{1,0:T(8,128)(2,1)S(1)} %bitcast.21), channel_id=1, source_target_pairs={{0,1},{1,0},{2,3},{3,2},{4,5},{5,4},{6,7},{7,6},{8,9},{9,8},{10,11... | collective-permute-start | bytes 2359304 | tf_op jit(solution)/shard_map/ppermute | solution.py:32
  84.0 4.4 %collective-permute-start.5 = (bf16[192,2048]{1,0:T(8,128)(2,1)}, bf16[192,2048]{1,0:T(8,128)(2,1)S(1)}, u32[]{:S(2)}, u32[]{:S(2)}) collective-permute-start(bf16[192,2048]{1,0:T(8,128)(2,1)} %collective-permute-done.w_y), channel_id=1, source_target_pairs={{0,1},{1,0},{2,3},{3,2},{4,5},{5,4},{6,7},{7,6},{8,9},{9,8},{10,11... | collective-permute-start | bytes 2359304 | tf_op jit(solution)/shard_map/ppermute | solution.py:32
  88.4 0.9 copy-start.2
  96.2 1.1 copy-start.3
  99.8 19.7 %collective-permute-start.6 = (bf16[64,768]{1,0:T(8,128)(2,1)S(1)}, bf16[64,768]{1,0:T(8,128)(2,1)S(1)}, u32[]{:S(2)}, u32[]{:S(2)}) collective-permute-start(bf16[64,768]{1,0:T(8,128)(2,1)S(1)} %get-tuple-element.21), channel_id=1, source_target_pairs={{0,16},{1,17},{2,18},{3,19},{4,20},{5,21},{6,22},{7,23},{8,24},{9,... | collective-permute-start | bytes 294920 | tf_op jit(solution)/shard_map/ppermute | solution.py:44
  103.6 16.3 %collective-permute-start.7 = (bf16[64,768]{1,0:T(8,128)(2,1)S(1)}, bf16[64,768]{1,0:T(8,128)(2,1)S(1)}, u32[]{:S(2)}, u32[]{:S(2)}) collective-permute-start(bf16[64,768]{1,0:T(8,128)(2,1)S(1)} %get-tuple-element.22), channel_id=1, source_target_pairs={{0,20},{1,21},{2,22},{3,23},{4,24},{5,25},{6,26},{7,27},{8,28},{9,... | collective-permute-start | bytes 294920 | tf_op jit(solution)/shard_map/ppermute | solution.py:44
  109.8 20.9 %collective-permute-start.8 = (bf16[64,768]{1,0:T(8,128)(2,1)S(1)}, bf16[64,768]{1,0:T(8,128)(2,1)S(1)}, u32[]{:S(2)}, u32[]{:S(2)}) collective-permute-start(bf16[64,768]{1,0:T(8,128)(2,1)S(1)} %get-tuple-element.23), channel_id=1, source_target_pairs={{0,24},{1,25},{2,26},{3,27},{4,28},{5,29},{6,30},{7,31},{8,16},{9,... | collective-permute-start | bytes 294920 | tf_op jit(solution)/shard_map/ppermute | solution.py:44
  113.7 18.9 %collective-permute-start.9 = (bf16[64,768]{1,0:T(8,128)(2,1)S(1)}, bf16[64,768]{1,0:T(8,128)(2,1)S(1)}, u32[]{:S(2)}, u32[]{:S(2)}) collective-permute-start(bf16[64,768]{1,0:T(8,128)(2,1)S(1)} %get-tuple-element.24), channel_id=1, source_target_pairs={{0,28},{1,29},{2,30},{3,31},{4,16},{5,17},{6,18},{7,19},{8,20},{9,... | collective-permute-start | bytes 294920 | tf_op jit(solution)/shard_map/ppermute | solution.py:44

commit v3 on v2

--- a/solution.py
+++ b/solution.py
@@ -184,6 +184,7 @@
             values[at + 32 : at + 96, 0:128] = old[k, :, 256:384]
     values[:, 128:256] = jnp.ones((2560, 128), jnp.bfloat16)
     scale = HD ** (-0.5) * math.log2(math.e)
+    stores = []
     for i in range(8):
         scores = lax.dot_general(
             query[128 * i : 128 * i + 128, :],
@@ -209,10 +210,13 @@
             dc, owner, y = i // 4, i % 4, n
             for to in range(NX):
                 staged[to, y * 2 + (c ^ dc), (owner - to) % NX] = result[64 * n : 64 * n + 64]
-    stores = []
-    for to in range(NX):
-        stores.append(pltpu.make_async_copy(staged.at[to], out.at[to], out_sems.at[to]))
-        stores[-1].start()
+        if owner == NX - 1:
+            for y in range(NY):
+                group = y * 2 + (c ^ dc)
+                stores.append(
+                    pltpu.make_async_copy(staged.at[:, group], out.at[:, group], out_sems.at[2 * dc + y])
+                )
+                stores[-1].start()
     for store in stores:
         store.wait()
 
@@ -235,13 +239,31 @@
     )(me, hide, own, own_old, sib, sib_old)
 
 
-def out_kernel(me_ref, heads, w_own, w_c, w_y, w_yc, mod, gathered, o0, o1, o2, o3, weight, held, w_sems, sems):
+def collect_kernel(me_ref, w_own, w_c, w_y, w_yc, weight, sems):
     x, y, c = place(me_ref)
-    parts = []
+    copies = []
     for i, (ref, dy, dc) in enumerate(((w_own, 0, 0), (w_c, 0, 1), (w_y, 1, 0), (w_yc, 1, 1))):
         at = pl.multiple_of(((y ^ dy) * 2 + (c ^ dc)) * 192, 64)
-        parts.append(pltpu.make_async_copy(ref, weight.at[pl.ds(at, 192), :], w_sems.at[i]))
-        parts[-1].start()
+        copies.append(pltpu.make_async_copy(ref, weight.at[pl.ds(at, 192), :], sems.at[i]))
+        copies[-1].start()
+    for copy in copies:
+        copy.wait()
+
+
+def collect(me, weights):
+    return pl.pallas_call(
+        collect_kernel,
+        out_shape=jax.ShapeDtypeStruct((768, 2048), jnp.bfloat16),
+        in_specs=[SCALAR] + [FAR] * 4,
+        out_specs=NEAR,
+        scratch_shapes=[pltpu.SemaphoreType.DMA((4,))],
+        compiler_params=params(4),
+        cost_estimate=cost(0.01),
+    )(me, *weights)
+
+
+def out_kernel(me_ref, heads, weight, mod, gathered, o0, o1, o2, o3, held, rows, sems, row_sems):
+    x, y, _ = place(me_ref)
     columns = pl.ds(pl.multiple_of(x * 768, 768), 768)
     loads = [
         pltpu.make_async_copy(
@@ -249,14 +271,22 @@
         )
         for i in range(4)
     ]
-    for load in loads:
+    parts = [
+        pltpu.make_async_copy(heads.at[4 * i : 4 * i + 4], rows.at[4 * i : 4 * i + 4], row_sems.at[i])
+        for i in range(4)
+    ]
+    for load in parts + loads:
         load.start()
-    rows = jnp.concatenate([heads[j] for j in range(16)], axis=-1)
-    for part in parts:
-        part.wait()
-    attn = lax.dot_general(
-        rows, weight[...], (((1,), (1,)), ((), ())), preferred_element_type=jnp.float32
-    ).astype(jnp.bfloat16).astype(jnp.float32)
+    attn = jnp.zeros((256, 768), jnp.float32)
+    for i in range(4):
+        parts[i].wait()
+        attn += lax.dot_general(
+            jnp.concatenate([rows[j] for j in range(4 * i, 4 * i + 4)], axis=-1),
+            weight[:, 512 * i : 512 * i + 512],
+            (((1,), (1,)), ((), ())),
+            preferred_element_type=jnp.float32,
+        )
+    attn = attn.astype(jnp.bfloat16).astype(jnp.float32)
     gate = mod[2:3, columns]
     for i, out in enumerate((o0, o1, o2, o3)):
         loads[i].wait()
@@ -264,22 +294,22 @@
         out[...] = (values + gate * attn[64 * i : 64 * i + 64, :]).astype(jnp.bfloat16)
 
 
-def project_out(me, heads, weights, mod, gathered):
+def project_out(me, heads, weight, mod, gathered):
     shape = jax.ShapeDtypeStruct((64, 768), jnp.bfloat16)
     return pl.pallas_call(
         out_kernel,
         out_shape=(shape,) * 4,
-        in_specs=[SCALAR, NEAR] + [FAR] * 4 + [NEAR, FAR],
+        in_specs=[SCALAR, FAR, NEAR, NEAR, FAR],
         out_specs=(NEAR,) * 4,
         scratch_shapes=[
-            pltpu.VMEM((768, 2048), jnp.bfloat16),
             pltpu.VMEM((4, 64, 768), jnp.bfloat16),
+            pltpu.VMEM((16, 256, HD), jnp.bfloat16),
             pltpu.SemaphoreType.DMA((4,)),
             pltpu.SemaphoreType.DMA((4,)),
         ],
-        compiler_params=params(32),
+        compiler_params=params(16),
         cost_estimate=cost(2),
-    )(me, heads, *weights, mod, gathered)
+    )(me, heads, weight, mod, gathered)
 
 
 def join_kernel(me_ref, p0, p1, p2, p3, out, sems):
@@ -329,9 +359,9 @@
     heads = attend(me, hide, own, own_old, sib, sib_old)
     (heads,) = following(out_y, heads)
     heads = lax.all_to_all(heads.reshape(16, 256, HD), "seq", 0, 0, tiled=True)
-    pieces = project_out(me, heads, (out_own, out_c, out_y, out_yc), mod, gathered)
-    pieces = [hand_on(piece, dx) for dx, piece in enumerate(pieces)]
-    return join(me, pieces)[None]
+    pieces = project_out(me, heads, collect(me, (out_own, out_c, out_y, out_yc)), mod, gathered)
+    arrived = {dx: hand_on(pieces[dx], dx) for dx in (2, 1, 3, 0)}
+    return join(me, [arrived[dx] for dx in range(NX)])[None]
 
 
 def solution(mesh):

time: 134 us -> 134 us (level)
  waiting for transfers between devices: 62.8 us -> 61.3 us
  Pallas kernels: 19.8 us -> 21.2 us
    pallas_call x1 -> x2, Pallas kernels: 2.46 us -> 3.99 us  [the longest x1 2.71 us: project_out(): pl.pallas_call(out_kernel, out_shape=(shape,) * 4, in_specs=[SCALAR, FAR,...]
    all_to_all x1, waiting for transfers between devices: 6.91 us -> 5.47 us  [on_device(): heads = lax.all_to_all(heads.reshape(16, 256, HD), 'seq', 0, 0, tiled=True)]
  transfers between devices with their start and end apart: 12 -> 12, of which waited for: 8 -> 8; matrix products, arithmetic and copies ran while one was open for 0% -> 0% of each run, Pallas kernels for 10% -> 11%
where the time goes in v3:
time: 134 us; the launch traced here: 133 us
  waiting for transfers between devices  61.3 us (46%)
  starting transfers between devices  48.3 us (36%)
  Pallas kernels  21.2 us (16%)
  local copies, waits for them, and re-layouts  1.37 us (1%)
    all_to_all x1, waiting for transfers between devices, on_device(): lax.all_to_all(sent, 'seq', 0, 0, tiled=True, axis_index_groups=LANES)  39.2 us
    ppermute x4, starting transfers between devices, hand_on(): return lax.ppermute(value, ('pipe', 'seq'), pairs)  19.2 us
    ppermute x4, waiting for transfers between devices, hand_on(): return lax.ppermute(value, ('pipe', 'seq'), pairs)  14.1 us
    ppermute x6, starting transfers between devices, shift(): return lax.ppermute(value, 'seq', pairs)  12.4 us
    all_to_all x1, starting transfers between devices, on_device(): lax.all_to_all(sent, 'seq', 0, 0, tiled=True, axis_index_groups=LANES)  10.6 us
    pallas_call x1, Pallas kernels, project_qkv(): pl.pallas_call(qkv_kernel, out_shape=(shape,) * 4, in_specs=[SCALAR, NEAR...  6.85 us
    all_to_all x1, starting transfers between devices, on_device(): heads = lax.all_to_all(heads.reshape(16, 256, HD), 'seq', 0, 0, tiled=True)  6.09 us
    all_to_all x1, waiting for transfers between devices, on_device(): heads = lax.all_to_all(heads.reshape(16, 256, HD), 'seq', 0, 0, tiled=True)  5.47 us
  transfers between devices with their start and end apart: 12, of which 8 were waited for; matrix products, arithmetic and copies ran while one was open for 0% of the time, Pallas kernels for 11%

profile of v3, /device:TPU:6, one launch (start us, length us, event | category | flops | bytes accessed | tf_op | source)
XLA Modules:
  0.0 133.1 jit_solution(7544980739721183772)
XLA Ops:
  0.0 3.2 %shard_map.73 = bf16[8,64,3840]{2,1,0:T(8,128)(2,1)} custom-call(bf16[64,3072]{1,0:T(8,128)(2,1)} %bitcast.27, bf16[192,2048]{1,0:T(8,128)(2,1)} %bitcast.26), custom_call_target="tpu_custom_call" | custom-call | flops 3000000000 | bytes 1 | tf_op jit(solution)/shard_map/pallas_call | solution.py:92
  3.2 10.6 %all-to-all-start = ((bf16[8,64,3840]{2,1,0:T(8,128)(2,1)}), bf16[8,64,3840]{2,1,0:T(8,128)(2,1)}, u32[]{:S(2)}, u32[]{:S(2)}) async-start(bf16[8,64,3840]{2,1,0:T(8,128)(2,1)} %shard_map.73), calls=%async_computation | async-start | bytes 7864320 | tf_op jit(solution)/shard_map/all_to_all | solution.py:350
  13.8 1.9 %collective-permute-start.1 = (bf16[3,3072,128]{2,1,0:T(8,128)(2,1)S(1)}, bf16[3,3072,128]{2,1,0:T(8,128)(2,1)}, u32[]{:S(2)}, u32[]{:S(2)}) collective-permute-start(bf16[3,3072,128]{2,1,0:T(8,128)(2,1)S(1)} %bitcast.18), channel_id=1, source_target_pairs={{0,1},{1,0},{2,3},{3,2},{4,5},{5,4},{6,7},{7,6},{8,9},{9,8},{10,11... | collective-permute-start | bytes 7077896 | tf_op jit(solution)/shard_map/ppermute | solution.py:32
  15.7 39.2 %all-to-all-done.gathered = bf16[8,64,3840]{2,1,0:T(8,128)(2,1)} async-done(((bf16[8,64,3840]{2,1,0:T(8,128)(2,1)}), bf16[8,64,3840]{2,1,0:T(8,128)(2,1)}, u32[]{:S(2)}, u32[]{:S(2)}) %all-to-all-start) | async-done | bytes 3932192 | tf_op jit(solution)/shard_map/all_to_all | solution.py:350
  54.9 1.9 %collective-permute-start = (bf16[192,2048]{1,0:T(8,128)(2,1)S(1)}, bf16[192,2048]{1,0:T(8,128)(2,1)}, u32[]{:S(2)}, u32[]{:S(2)}) collective-permute-start(bf16[192,2048]{1,0:T(8,128)(2,1)S(1)} %bitcast.20), channel_id=1, source_target_pairs={{0,2},{1,3},{2,0},{3,1},{4,6},{5,7},{6,4},{7,5},{8,10},{9,11},{10,... | collective-permute-start | bytes 2359304 | tf_op jit(solution)/shard_map/ppermute | solution.py:32
  56.9 1.7 %shard_map.74.weight = bf16[6,3072,128]{2,1,0:T(8,128)(2,1)S(1)} custom-call(bf16[3,3072,128]{2,1,0:T(8,128)(2,1)S(1)} %bitcast.19, bf16[3,3072,128]{2,1,0:T(8,128)(2,1)} %collective-permute-done.1.w_sib), custom_call_target="tpu_custom_call" | custom-call | flops 10000000 | bytes 1 | tf_op jit(solution)/shard_map/pallas_call | solution.py:119
  58.6 6.8 %shard_map.75 = (bf16[8,64,384]{2,1,0:T(8,128)(2,1)S(1)}, bf16[8,64,384]{2,1,0:T(8,128)(2,1)S(1)}, bf16[8,64,384]{2,1,0:T(8,128)(2,1)}, bf16[8,64,384]{2,1,0:T(8,128)(2,1)S(1)}) custom-call(s32[1]{0:T(128)} %bitcast.me_ref, bf16[8,64,3840]{2,1,0:T(8,128)(2,1)} %all-to-all-done.gathered, f32[3,3072]{1,0:T(4,128)S(1)} %bitcast.23, ...), custom_call_target="tpu_custom_call" | custom-call | flops 10000000 | bytes 1 | tf_op jit(solution)/shard_map/pallas_call | solution.py:161
  65.4 1.9 %collective-permute-start.2 = (bf16[8,64,384]{2,1,0:T(8,128)(2,1)}, bf16[8,64,384]{2,1,0:T(8,128)(2,1)S(1)}, u32[]{:S(2)}, u32[]{:S(2)}) collective-permute-start(bf16[8,64,384]{2,1,0:T(8,128)(2,1)} %get-tuple-element.18), channel_id=1, source_target_pairs={{0,1},{1,0},{2,3},{3,2},{4,5},{5,4},{6,7},{7,6},{8,9},{9,8},{10,11... | collective-permute-start | bytes 1179656 | tf_op jit(solution)/shard_map/ppermute | solution.py:32
  67.4 2.4 %collective-permute-start.3 = (bf16[8,64,384]{2,1,0:T(8,128)(2,1)S(1)}, bf16[8,64,384]{2,1,0:T(8,128)(2,1)S(1)}, u32[]{:S(2)}, u32[]{:S(2)}) collective-permute-start(bf16[8,64,384]{2,1,0:T(8,128)(2,1)S(1)} %get-tuple-element.19), channel_id=1, source_target_pairs={{0,1},{1,0},{2,3},{3,2},{4,5},{5,4},{6,7},{7,6},{8,9},{9,8},{10,11... | collective-permute-start | bytes 1179656 | tf_op jit(solution)/shard_map/ppermute | solution.py:32
  71.1 4.7 %shard_map.76 = bf16[4,4,4,64,128]{4,3,2,1,0:T(8,128)(2,1)} custom-call(s32[1]{0:T(128)} %bitcast.me_ref, f32[1,1536]{1,0:T(1,128)S(1)} %select_n.25.hide, bf16[8,64,384]{2,1,0:T(8,128)(2,1)S(1)} %get-tuple-element.16.own, bf16[8,64,384]{2,1,0:T(8,128)(2,1)S(1)} %get-tuple-element.17.own_old, bf16[8,64,384]{2,1,0:T(8,128)(2,1)S(1)} %collective-permute-done.2.sib, ...), custom_call_target="tpu_custom_call" | custom-call | flops 10000000 | bytes 1 | tf_op jit(solution)/shard_map/pallas_call | solution.py:225
  75.8 6.1 %all-to-all-start.1 = ((bf16[16,256,128]{2,1,0:T(8,128)(2,1)}), bf16[16,256,128]{2,1,0:T(8,128)(2,1)}, u32[]{:S(2)}, u32[]{:S(2)}) async-start(bf16[16,256,128]{2,1,0:T(8,128)(2,1)} %bitcast.10), calls=%async_computation.1 | async-start | bytes 2097152 | tf_op jit(solution)/shard_map/all_to_all | solution.py:361
  81.9 2.0 %collective-permute-start.4 = (bf16[192,2048]{1,0:T(8,128)(2,1)S(1)}, bf16[192,2048]{1,0:T(8,128)(2,1)S(1)}, u32[]{:S(2)}, u32[]{:S(2)}) collective-permute-start(bf16[192,2048]{1,0:T(8,128)(2,1)S(1)} %bitcast.21), channel_id=1, source_target_pairs={{0,1},{1,0},{2,3},{3,2},{4,5},{5,4},{6,7},{7,6},{8,9},{9,8},{10,11... | collective-permute-start | bytes 2359304 | tf_op jit(solution)/shard_map/ppermute | solution.py:32
  83.9 2.3 %collective-permute-start.5 = (bf16[192,2048]{1,0:T(8,128)(2,1)}, bf16[192,2048]{1,0:T(8,128)(2,1)S(1)}, u32[]{:S(2)}, u32[]{:S(2)}) collective-permute-start(bf16[192,2048]{1,0:T(8,128)(2,1)} %collective-permute-done.w_y), channel_id=1, source_target_pairs={{0,1},{1,0},{2,3},{3,2},{4,5},{5,4},{6,7},{7,6},{8,9},{9,8},{10,11... | collective-permute-start | bytes 2359304 | tf_op jit(solution)/shard_map/ppermute | solution.py:32
  86.2 2.1 %collective-permute-done.5.w_yc = bf16[192,2048]{1,0:T(8,128)(2,1)S(1)} collective-permute-done((bf16[192,2048]{1,0:T(8,128)(2,1)}, bf16[192,2048]{1,0:T(8,128)(2,1)S(1)}, u32[]{:S(2)}, u32[]{:S(2)}) %collective-permute-start.5) | collective-permute-done | bytes 786464 | tf_op jit(solution)/shard_map/ppermute | solution.py:32
  88.3 1.1 copy-done.2
  89.5 1.3 shard_map.77.weight
  90.7 5.5 %all-to-all-done.1.heads = bf16[16,256,128]{2,1,0:T(8,128)(2,1)} async-done(((bf16[16,256,128]{2,1,0:T(8,128)(2,1)}), bf16[16,256,128]{2,1,0:T(8,128)(2,1)}, u32[]{:S(2)}, u32[]{:S(2)}) %all-to-all-start.1) | async-done | bytes 1048608 | tf_op jit(solution)/shard_map/all_to_all | solution.py:361
  96.2 2.7 %shard_map.78 = (bf16[64,768]{1,0:T(8,128)(2,1)S(1)}, bf16[64,768]{1,0:T(8,128)(2,1)S(1)}, bf16[64,768]{1,0:T(8,128)(2,1)S(1)}, bf16[64,768]{1,0:T(8,128)(2,1)S(1)}) custom-call(s32[1]{0:T(128)} %bitcast.me_ref, bf16[16,256,128]{2,1,0:T(8,128)(2,1)} %all-to-all-done.1.heads, bf16[768,2048]{1,0:T(8,128)(2,1)S(1)} %shard_map.77.weight, ...), custom_call_target="tpu_custom_call" | custom-call | flops 2000000000 | bytes 1 | tf_op jit(solution)/shard_map/pallas_call | solution.py:299
  98.9 4.3 %collective-permute-start.6 = (bf16[64,768]{1,0:T(8,128)(2,1)S(1)}, bf16[64,768]{1,0:T(8,128)(2,1)S(1)}, u32[]{:S(2)}, u32[]{:S(2)}) collective-permute-start(bf16[64,768]{1,0:T(8,128)(2,1)S(1)} %get-tuple-element.21), channel_id=1, source_target_pairs={{0,16},{1,17},{2,18},{3,19},{4,20},{5,21},{6,22},{7,23},{8,24},{9,... | collective-permute-start | bytes 294920 | tf_op jit(solution)/shard_map/ppermute | solution.py:44
  103.2 6.2 %collective-permute-start.7 = (bf16[64,768]{1,0:T(8,128)(2,1)S(1)}, bf16[64,768]{1,0:T(8,128)(2,1)S(1)}, u32[]{:S(2)}, u32[]{:S(2)}) collective-permute-start(bf16[64,768]{1,0:T(8,128)(2,1)S(1)} %get-tuple-element.22), channel_id=1, source_target_pairs={{0,20},{1,21},{2,22},{3,23},{4,24},{5,25},{6,26},{7,27},{8,28},{9,... | collective-permute-start | bytes 294920 | tf_op jit(solution)/shard_map/ppermute | solution.py:44
  109.4 3.9 %collective-permute-start.8 = (bf16[64,768]{1,0:T(8,128)(2,1)S(1)}, bf16[64,768]{1,0:T(8,128)(2,1)S(1)}, u32[]{:S(2)}, u32[]{:S(2)}) collective-permute-start(bf16[64,768]{1,0:T(8,128)(2,1)S(1)} %get-tuple-element.23), channel_id=1, source_target_pairs={{0,24},{1,25},{2,26},{3,27},{4,28},{5,29},{6,30},{7,31},{8,16},{9,... | collective-permute-start | bytes 294920 | tf_op jit(solution)/shard_map/ppermute | solution.py:44
  113.4 4.8 %collective-permute-start.9 = (bf16[64,768]{1,0:T(8,128)(2,1)S(1)}, bf16[64,768]{1,0:T(8,128)(2,1)S(1)}, u32[]{:S(2)}, u32[]{:S(2)}) collective-permute-start(bf16[64,768]{1,0:T(8,128)(2,1)S(1)} %get-tuple-element.24), channel_id=1, source_target_pairs={{0,28},{1,29},{2,30},{3,31},{4,16},{5,17},{6,18},{7,19},{8,20},{9,... | collective-permute-start | bytes 294920 | tf_op jit(solution)/shard_map/ppermute | solution.py:44
  119.5 10.8 %collective-permute-done.8.p2 = bf16[64,768]{1,0:T(8,128)(2,1)S(1)} collective-permute-done((bf16[64,768]{1,0:T(8,128)(2,1)S(1)}, bf16[64,768]{1,0:T(8,128)(2,1)S(1)}, u32[]{:S(2)}, u32[]{:S(2)}) %collective-permute-start.8) | collective-permute-done | bytes 98336 | tf_op jit(solution)/shard_map/ppermute | solution.py:44
  130.4 1.9 %collective-permute-done.9.p3 = bf16[64,768]{1,0:T(8,128)(2,1)S(1)} collective-permute-done((bf16[64,768]{1,0:T(8,128)(2,1)S(1)}, bf16[64,768]{1,0:T(8,128)(2,1)S(1)}, u32[]{:S(2)}, u32[]{:S(2)}) %collective-permute-start.9) | collective-permute-done | bytes 98336 | tf_op jit(solution)/shard_map/ppermute | solution.py:44
  (23 shorter events, 2.8 us)
Async XLA Ops:
  3.2 10.6 %copy-start = (bf16[1,3072,3,128]{3,1,2,0:T(8,128)(2,1)S(1)}, bf16[1,3072,3,128]{3,1,2,0:T(8,128)(2,1)}, u32[]{:S(2)}) copy-start(bf16[1,3072,3,128]{3,1,2,0:T(8,128)(2,1)} %param.9) | copy-start | bytes 7077892
  3.2 51.7 %copy-start.1 = (bf16[1,2048,192]{1,2,0:T(8,128)(2,1)S(1)}, bf16[1,2048,192]{1,2,0:T(8,128)(2,1)}, u32[]{:S(2)}) copy-start(bf16[1,2048,192]{1,2,0:T(8,128)(2,1)} %param.10) | copy-start | bytes 2359300
  3.2 53.6 %copy-start.3 = (f32[1,3,3072]{2,0,1:T(1,128)S(1)}, f32[1,3,3072]{2,0,1:T(1,128)}, u32[]{:S(2)}) copy-start(f32[1,3,3072]{2,0,1:T(1,128)} %param.8) | copy-start | bytes 110596
  3.2 51.7 %all-to-all-start = ((bf16[8,64,3840]{2,1,0:T(8,128)(2,1)}), bf16[8,64,3840]{2,1,0:T(8,128)(2,1)}, u32[]{:S(2)}, u32[]{:S(2)}) async-start(bf16[8,64,3840]{2,1,0:T(8,128)(2,1)} %shard_map.73), calls=%async_computation | async-start | bytes 7864320 | tf_op jit(solution)/shard_map/all_to_all | solution.py:350
  13.8 43.1 %collective-permute-start.1 = (bf16[3,3072,128]{2,1,0:T(8,128)(2,1)S(1)}, bf16[3,3072,128]{2,1,0:T(8,128)(2,1)}, u32[]{:S(2)}, u32[]{:S(2)}) collective-permute-start(bf16[3,3072,128]{2,1,0:T(8,128)(2,1)S(1)} %bitcast.18), channel_id=1, source_target_pairs={{0,1},{1,0},{2,3},{3,2},{4,5},{5,4},{6,7},{7,6},{8,9},{9,8},{10,11... | collective-permute-start | bytes 7077896 | tf_op jit(solution)/shard_map/ppermute | solution.py:32
  54.9 20.9 %collective-permute-start = (bf16[192,2048]{1,0:T(8,128)(2,1)S(1)}, bf16[192,2048]{1,0:T(8,128)(2,1)}, u32[]{:S(2)}, u32[]{:S(2)}) collective-permute-start(bf16[192,2048]{1,0:T(8,128)(2,1)S(1)} %bitcast.20), channel_id=1, source_target_pairs={{0,2},{1,3},{2,0},{3,1},{4,6},{5,7},{6,4},{7,5},{8,10},{9,11},{10,... | collective-permute-start | bytes 2359304 | tf_op jit(solution)/shard_map/ppermute | solution.py:32
  58.6 11.2 %copy-start.4 = (s32[1536]{0:T(1024)S(1)}, s32[1536]{0:T(1024)}, u32[]{:S(2)}) copy-start(s32[1536]{0:T(1024)} %param.13) | copy-start | bytes 18436
  65.4 5.2 %collective-permute-start.2 = (bf16[8,64,384]{2,1,0:T(8,128)(2,1)}, bf16[8,64,384]{2,1,0:T(8,128)(2,1)S(1)}, u32[]{:S(2)}, u32[]{:S(2)}) collective-permute-start(bf16[8,64,384]{2,1,0:T(8,128)(2,1)} %get-tuple-element.18), channel_id=1, source_target_pairs={{0,1},{1,0},{2,3},{3,2},{4,5},{5,4},{6,7},{7,6},{8,9},{9,8},{10,11... | collective-permute-start | bytes 1179656 | tf_op jit(solution)/shard_map/ppermute | solution.py:32
  67.4 3.7 %collective-permute-start.3 = (bf16[8,64,384]{2,1,0:T(8,128)(2,1)S(1)}, bf16[8,64,384]{2,1,0:T(8,128)(2,1)S(1)}, u32[]{:S(2)}, u32[]{:S(2)}) collective-permute-start(bf16[8,64,384]{2,1,0:T(8,128)(2,1)S(1)} %get-tuple-element.19), channel_id=1, source_target_pairs={{0,1},{1,0},{2,3},{3,2},{4,5},{5,4},{6,7},{7,6},{8,9},{9,8},{10,11... | collective-permute-start | bytes 1179656 | tf_op jit(solution)/shard_map/ppermute | solution.py:32
  75.8 20.4 %all-to-all-start.1 = ((bf16[16,256,128]{2,1,0:T(8,128)(2,1)}), bf16[16,256,128]{2,1,0:T(8,128)(2,1)}, u32[]{:S(2)}, u32[]{:S(2)}) async-start(bf16[16,256,128]{2,1,0:T(8,128)(2,1)} %bitcast.10), calls=%async_computation.1 | async-start | bytes 2097152 | tf_op jit(solution)/shard_map/all_to_all | solution.py:361
  81.9 4.3 %collective-permute-start.4 = (bf16[192,2048]{1,0:T(8,128)(2,1)S(1)}, bf16[192,2048]{1,0:T(8,128)(2,1)S(1)}, u32[]{:S(2)}, u32[]{:S(2)}) collective-permute-start(bf16[192,2048]{1,0:T(8,128)(2,1)S(1)} %bitcast.21), channel_id=1, source_target_pairs={{0,1},{1,0},{2,3},{3,2},{4,5},{5,4},{6,7},{7,6},{8,9},{9,8},{10,11... | collective-permute-start | bytes 2359304 | tf_op jit(solution)/shard_map/ppermute | solution.py:32
  83.9 4.4 %collective-permute-start.5 = (bf16[192,2048]{1,0:T(8,128)(2,1)}, bf16[192,2048]{1,0:T(8,128)(2,1)S(1)}, u32[]{:S(2)}, u32[]{:S(2)}) collective-permute-start(bf16[192,2048]{1,0:T(8,128)(2,1)} %collective-permute-done.w_y), channel_id=1, source_target_pairs={{0,1},{1,0},{2,3},{3,2},{4,5},{5,4},{6,7},{7,6},{8,9},{9,8},{10,11... | collective-permute-start | bytes 2359304 | tf_op jit(solution)/shard_map/ppermute | solution.py:32
  88.3 1.1 copy-start.2
  98.9 20.2 %collective-permute-start.6 = (bf16[64,768]{1,0:T(8,128)(2,1)S(1)}, bf16[64,768]{1,0:T(8,128)(2,1)S(1)}, u32[]{:S(2)}, u32[]{:S(2)}) collective-permute-start(bf16[64,768]{1,0:T(8,128)(2,1)S(1)} %get-tuple-element.21), channel_id=1, source_target_pairs={{0,16},{1,17},{2,18},{3,19},{4,20},{5,21},{6,22},{7,23},{8,24},{9,... | collective-permute-start | bytes 294920 | tf_op jit(solution)/shard_map/ppermute | solution.py:44
  103.2 16.3 %collective-permute-start.7 = (bf16[64,768]{1,0:T(8,128)(2,1)S(1)}, bf16[64,768]{1,0:T(8,128)(2,1)S(1)}, u32[]{:S(2)}, u32[]{:S(2)}) collective-permute-start(bf16[64,768]{1,0:T(8,128)(2,1)S(1)} %get-tuple-element.22), channel_id=1, source_target_pairs={{0,20},{1,21},{2,22},{3,23},{4,24},{5,25},{6,26},{7,27},{8,28},{9,... | collective-permute-start | bytes 294920 | tf_op jit(solution)/shard_map/ppermute | solution.py:44
  109.4 20.9 %collective-permute-start.8 = (bf16[64,768]{1,0:T(8,128)(2,1)S(1)}, bf16[64,768]{1,0:T(8,128)(2,1)S(1)}, u32[]{:S(2)}, u32[]{:S(2)}) collective-permute-start(bf16[64,768]{1,0:T(8,128)(2,1)S(1)} %get-tuple-element.23), channel_id=1, source_target_pairs={{0,24},{1,25},{2,26},{3,27},{4,28},{5,29},{6,30},{7,31},{8,16},{9,... | collective-permute-start | bytes 294920 | tf_op jit(solution)/shard_map/ppermute | solution.py:44
  113.4 18.9 %collective-permute-start.9 = (bf16[64,768]{1,0:T(8,128)(2,1)S(1)}, bf16[64,768]{1,0:T(8,128)(2,1)S(1)}, u32[]{:S(2)}, u32[]{:S(2)}) collective-permute-start(bf16[64,768]{1,0:T(8,128)(2,1)S(1)} %get-tuple-element.24), channel_id=1, source_target_pairs={{0,28},{1,29},{2,30},{3,31},{4,16},{5,17},{6,18},{7,19},{8,20},{9,... | collective-permute-start | bytes 294920 | tf_op jit(solution)/shard_map/ppermute | solution.py:44

commit v4 on v3

--- a/solution.py
+++ b/solution.py
@@ -262,14 +262,14 @@
     )(me, *weights)
 
 
-def out_kernel(me_ref, heads, weight, mod, gathered, o0, o1, o2, o3, held, rows, sems, row_sems):
+def out_kernel(me_ref, heads, weight, gate, gathered, o0, o1, o2, o3, rows, kept, row_sems, kept_sems):
     x, y, _ = place(me_ref)
     columns = pl.ds(pl.multiple_of(x * 768, 768), 768)
     loads = [
         pltpu.make_async_copy(
-            gathered.at[((x + i) & 3) * 2 + y, :, columns], held.at[i], sems.at[i]
-        )
-        for i in range(4)
+            gathered.at[((x + i) & 3) * 2 + y, :, columns], kept.at[i], kept_sems.at[i]
+        )
+        for i in range(NX)
     ]
     parts = [
         pltpu.make_async_copy(heads.at[4 * i : 4 * i + 4], rows.at[4 * i : 4 * i + 4], row_sems.at[i])
@@ -287,14 +287,13 @@
             preferred_element_type=jnp.float32,
         )
     attn = attn.astype(jnp.bfloat16).astype(jnp.float32)
-    gate = mod[2:3, columns]
     for i, out in enumerate((o0, o1, o2, o3)):
         loads[i].wait()
-        values = held[i].astype(jnp.float32)
-        out[...] = (values + gate * attn[64 * i : 64 * i + 64, :]).astype(jnp.bfloat16)
-
-
-def project_out(me, heads, weight, mod, gathered):
+        values = kept[i].astype(jnp.float32)
+        out[...] = (values + gate[...] * attn[64 * i : 64 * i + 64, :]).astype(jnp.bfloat16)
+
+
+def project_out(me, heads, weight, gate, gathered):
     shape = jax.ShapeDtypeStruct((64, 768), jnp.bfloat16)
     return pl.pallas_call(
         out_kernel,
@@ -302,14 +301,14 @@
         in_specs=[SCALAR, FAR, NEAR, NEAR, FAR],
         out_specs=(NEAR,) * 4,
         scratch_shapes=[
-            pltpu.VMEM((4, 64, 768), jnp.bfloat16),
             pltpu.VMEM((16, 256, HD), jnp.bfloat16),
+            pltpu.VMEM((NX, 64, 768), jnp.bfloat16),
             pltpu.SemaphoreType.DMA((4,)),
-            pltpu.SemaphoreType.DMA((4,)),
+            pltpu.SemaphoreType.DMA((NX,)),
         ],
         compiler_params=params(16),
         cost_estimate=cost(2),
-    )(me, heads, weight, mod, gathered)
+    )(me, heads, weight, gate, gathered)
 
 
 def join_kernel(me_ref, p0, p1, p2, p3, out, sems):
@@ -359,7 +358,9 @@
     heads = attend(me, hide, own, own_old, sib, sib_old)
     (heads,) = following(out_y, heads)
     heads = lax.all_to_all(heads.reshape(16, 256, HD), "seq", 0, 0, tiled=True)
-    pieces = project_out(me, heads, collect(me, (out_own, out_c, out_y, out_yc)), mod, gathered)
+    weight = collect(me, (out_own, out_c, out_y, out_yc))
+    gate = lax.dynamic_slice(mod, (2, index // (NY * NC) * 768), (1, 768))
+    pieces = project_out(me, heads, weight, gate, gathered)
     arrived = {dx: hand_on(pieces[dx], dx) for dx in (2, 1, 3, 0)}
     return join(me, [arrived[dx] for dx in range(NX)])[None]
 

time: 134 us -> 133 us (level)
  local copies, waits for them, and re-layouts: 1.37 us -> 6.17 us
  waiting for transfers between devices: 61.3 us -> 56.5 us
    unnamed x11 -> x19, local copies, waits for them, and re-layouts: 1.17 us -> 5.28 us
    all_to_all x1, waiting for transfers between devices: 5.47 us -> 2.23 us  [on_device(): heads = lax.all_to_all(heads.reshape(16, 256, HD), 'seq', 0, 0, tiled=True)]
    ppermute x6, waiting for transfers between devices: 2.54 us -> 0.96 us  [shift(): return lax.ppermute(value, 'seq', pairs)]
  transfers between devices with their start and end apart: 12 -> 12, of which waited for: 8 -> 8; matrix products, arithmetic and copies ran while one was open for 0% -> 1% of each run, Pallas kernels for 11% -> 10%
where the time goes in v4:
time: 133 us; the launch traced here: 132 us
  waiting for transfers between devices  56.5 us (42%)
  starting transfers between devices  48.3 us (36%)
  Pallas kernels  20.5 us (15%)
  local copies, waits for them, and re-layouts  6.17 us (5%)
    all_to_all x1, waiting for transfers between devices, on_device(): lax.all_to_all(sent, 'seq', 0, 0, tiled=True, axis_index_groups=LANES)  39.2 us
    ppermute x4, starting transfers between devices, hand_on(): return lax.ppermute(value, ('pipe', 'seq'), pairs)  19.2 us
    ppermute x4, waiting for transfers between devices, hand_on(): return lax.ppermute(value, ('pipe', 'seq'), pairs)  14.1 us
    ppermute x6, starting transfers between devices, shift(): return lax.ppermute(value, 'seq', pairs)  12.5 us
    all_to_all x1, starting transfers between devices, on_device(): lax.all_to_all(sent, 'seq', 0, 0, tiled=True, axis_index_groups=LANES)  10.6 us
    pallas_call x1, Pallas kernels, project_qkv(): pl.pallas_call(qkv_kernel, out_shape=(shape,) * 4, in_specs=[SCALAR, NEAR...  6.1 us
    all_to_all x1, starting transfers between devices, on_device(): heads = lax.all_to_all(heads.reshape(16, 256, HD), 'seq', 0, 0, tiled=True)  6.08 us
    unnamed x19, local copies, waits for them, and re-layouts  5.28 us
  transfers between devices with their start and end apart: 12, of which 8 were waited for; matrix products, arithmetic and copies ran while one was open for 1% of the time, Pallas kernels for 10%

profile of v4, /device:TPU:6, one launch (start us, length us, event | category | flops | bytes accessed | tf_op | source)
XLA Modules:
  0.0 132.4 jit_solution(13219538210473466324)
XLA Ops:
  0.0 3.2 %shard_map.73 = bf16[8,64,3840]{2,1,0:T(8,128)(2,1)} custom-call(bf16[64,3072]{1,0:T(8,128)(2,1)} %bitcast.28, bf16[192,2048]{1,0:T(8,128)(2,1)} %bitcast.27), custom_call_target="tpu_custom_call" | custom-call | flops 3000000000 | bytes 1 | tf_op jit(solution)/shard_map/pallas_call | solution.py:92
  3.3 10.6 %all-to-all-start = ((bf16[8,64,3840]{2,1,0:T(8,128)(2,1)}), bf16[8,64,3840]{2,1,0:T(8,128)(2,1)}, u32[]{:S(2)}, u32[]{:S(2)}) async-start(bf16[8,64,3840]{2,1,0:T(8,128)(2,1)} %shard_map.73), calls=%async_computation | async-start | bytes 7864320 | tf_op jit(solution)/shard_map/all_to_all | solution.py:349
  13.8 1.9 %collective-permute-start.1 = (bf16[3,3072,128]{2,1,0:T(8,128)(2,1)S(1)}, bf16[3,3072,128]{2,1,0:T(8,128)(2,1)}, u32[]{:S(2)}, u32[]{:S(2)}) collective-permute-start(bf16[3,3072,128]{2,1,0:T(8,128)(2,1)S(1)} %bitcast.20), channel_id=1, source_target_pairs={{0,1},{1,0},{2,3},{3,2},{4,5},{5,4},{6,7},{7,6},{8,9},{9,8},{10,11... | collective-permute-start | bytes 7077896 | tf_op jit(solution)/shard_map/ppermute | solution.py:32
  15.8 39.2 %all-to-all-done.gathered = bf16[8,64,3840]{2,1,0:T(8,128)(2,1)} async-done(((bf16[8,64,3840]{2,1,0:T(8,128)(2,1)}), bf16[8,64,3840]{2,1,0:T(8,128)(2,1)}, u32[]{:S(2)}, u32[]{:S(2)}) %all-to-all-start) | async-done | bytes 3932192 | tf_op jit(solution)/shard_map/all_to_all | solution.py:349
  54.9 1.9 %collective-permute-start = (bf16[192,2048]{1,0:T(8,128)(2,1)S(1)}, bf16[192,2048]{1,0:T(8,128)(2,1)}, u32[]{:S(2)}, u32[]{:S(2)}) collective-permute-start(bf16[192,2048]{1,0:T(8,128)(2,1)S(1)} %bitcast.22), channel_id=1, source_target_pairs={{0,2},{1,3},{2,0},{3,1},{4,6},{5,7},{6,4},{7,5},{8,10},{9,11},{10,... | collective-permute-start | bytes 2359304 | tf_op jit(solution)/shard_map/ppermute | solution.py:32
  56.9 1.7 %shard_map.74.weight = bf16[6,3072,128]{2,1,0:T(8,128)(2,1)S(1)} custom-call(bf16[3,3072,128]{2,1,0:T(8,128)(2,1)S(1)} %bitcast.21, bf16[3,3072,128]{2,1,0:T(8,128)(2,1)} %collective-permute-done.1.w_sib), custom_call_target="tpu_custom_call" | custom-call | flops 10000000 | bytes 1 | tf_op jit(solution)/shard_map/pallas_call | solution.py:119
  58.6 6.1 %shard_map.75 = (bf16[8,64,384]{2,1,0:T(8,128)(2,1)S(1)}, bf16[8,64,384]{2,1,0:T(8,128)(2,1)S(1)}, bf16[8,64,384]{2,1,0:T(8,128)(2,1)S(1)}, bf16[8,64,384]{2,1,0:T(8,128)(2,1)S(1)}) custom-call(s32[1]{0:T(128)} %bitcast.me_ref, bf16[8,64,3840]{2,1,0:T(8,128)(2,1)} %all-to-all-done.gathered, f32[3,3072]{1,0:T(4,128)S(1)} %bitcast.25, ...), custom_call_target="tpu_custom_call" | custom-call | flops 10000000 | bytes 1 | tf_op jit(solution)/shard_map/pallas_call | solution.py:161
  64.7 1.9 %collective-permute-start.2 = (bf16[8,64,384]{2,1,0:T(8,128)(2,1)S(1)}, bf16[8,64,384]{2,1,0:T(8,128)(2,1)S(1)}, u32[]{:S(2)}, u32[]{:S(2)}) collective-permute-start(bf16[8,64,384]{2,1,0:T(8,128)(2,1)S(1)} %get-tuple-element.18), channel_id=1, source_target_pairs={{0,1},{1,0},{2,3},{3,2},{4,5},{5,4},{6,7},{7,6},{8,9},{9,8},{10,11... | collective-permute-start | bytes 1179656 | tf_op jit(solution)/shard_map/ppermute | solution.py:32
  66.7 2.4 %collective-permute-start.3 = (bf16[8,64,384]{2,1,0:T(8,128)(2,1)S(1)}, bf16[8,64,384]{2,1,0:T(8,128)(2,1)S(1)}, u32[]{:S(2)}, u32[]{:S(2)}) collective-permute-start(bf16[8,64,384]{2,1,0:T(8,128)(2,1)S(1)} %get-tuple-element.19), channel_id=1, source_target_pairs={{0,1},{1,0},{2,3},{3,2},{4,5},{5,4},{6,7},{7,6},{8,9},{9,8},{10,11... | collective-permute-start | bytes 1179656 | tf_op jit(solution)/shard_map/ppermute | solution.py:32
  70.4 4.7 %shard_map.76 = bf16[4,4,4,64,128]{4,3,2,1,0:T(8,128)(2,1)} custom-call(s32[1]{0:T(128)} %bitcast.me_ref, f32[1,1536]{1,0:T(1,128)S(1)} %select_n.32.hide, bf16[8,64,384]{2,1,0:T(8,128)(2,1)S(1)} %get-tuple-element.16.own, bf16[8,64,384]{2,1,0:T(8,128)(2,1)S(1)} %get-tuple-element.17.own_old, bf16[8,64,384]{2,1,0:T(8,128)(2,1)S(1)} %collective-permute-done.2.sib, ...), custom_call_target="tpu_custom_call" | custom-call | flops 10000000 | bytes 1 | tf_op jit(solution)/shard_map/pallas_call | solution.py:225
  75.1 6.1 %all-to-all-start.1 = ((bf16[16,256,128]{2,1,0:T(8,128)(2,1)}), bf16[16,256,128]{2,1,0:T(8,128)(2,1)}, u32[]{:S(2)}, u32[]{:S(2)}) async-start(bf16[16,256,128]{2,1,0:T(8,128)(2,1)} %bitcast.10), calls=%async_computation.1 | async-start | bytes 2097152 | tf_op jit(solution)/shard_map/all_to_all | solution.py:360
  81.2 2.0 %collective-permute-start.4 = (bf16[192,2048]{1,0:T(8,128)(2,1)S(1)}, bf16[192,2048]{1,0:T(8,128)(2,1)S(1)}, u32[]{:S(2)}, u32[]{:S(2)}) collective-permute-start(bf16[192,2048]{1,0:T(8,128)(2,1)S(1)} %bitcast.23), channel_id=1, source_target_pairs={{0,1},{1,0},{2,3},{3,2},{4,5},{5,4},{6,7},{7,6},{8,9},{9,8},{10,11... | collective-permute-start | bytes 2359304 | tf_op jit(solution)/shard_map/ppermute | solution.py:32
  83.2 2.3 %collective-permute-start.5 = (bf16[192,2048]{1,0:T(8,128)(2,1)}, bf16[192,2048]{1,0:T(8,128)(2,1)S(1)}, u32[]{:S(2)}, u32[]{:S(2)}) collective-permute-start(bf16[192,2048]{1,0:T(8,128)(2,1)} %collective-permute-done.w_y), channel_id=1, source_target_pairs={{0,1},{1,0},{2,3},{3,2},{4,5},{5,4},{6,7},{7,6},{8,9},{9,8},{10,11... | collective-permute-start | bytes 2359304 | tf_op jit(solution)/shard_map/ppermute | solution.py:32
  88.6 1.1 copy-done.2
  90.9 1.1 copy-done.6
  92.0 1.3 shard_map.77.weight
  93.3 2.2 %all-to-all-done.1.heads = bf16[16,256,128]{2,1,0:T(8,128)(2,1)} async-done(((bf16[16,256,128]{2,1,0:T(8,128)(2,1)}), bf16[16,256,128]{2,1,0:T(8,128)(2,1)}, u32[]{:S(2)}, u32[]{:S(2)}) %all-to-all-start.1) | async-done | bytes 1048608 | tf_op jit(solution)/shard_map/all_to_all | solution.py:360
  95.5 2.7 %shard_map.78 = (bf16[64,768]{1,0:T(8,128)(2,1)S(1)}, bf16[64,768]{1,0:T(8,128)(2,1)S(1)}, bf16[64,768]{1,0:T(8,128)(2,1)S(1)}, bf16[64,768]{1,0:T(8,128)(2,1)S(1)}) custom-call(s32[1]{0:T(128)} %bitcast.me_ref, bf16[16,256,128]{2,1,0:T(8,128)(2,1)} %all-to-all-done.1.heads, bf16[768,2048]{1,0:T(8,128)(2,1)S(1)} %shard_map.77.weight, ...), custom_call_target="tpu_custom_call" | custom-call | flops 2000000000 | bytes 1 | tf_op jit(solution)/shard_map/pallas_call | solution.py:298
  98.2 4.3 %collective-permute-start.6 = (bf16[64,768]{1,0:T(8,128)(2,1)S(1)}, bf16[64,768]{1,0:T(8,128)(2,1)S(1)}, u32[]{:S(2)}, u32[]{:S(2)}) collective-permute-start(bf16[64,768]{1,0:T(8,128)(2,1)S(1)} %get-tuple-element.21), channel_id=1, source_target_pairs={{0,16},{1,17},{2,18},{3,19},{4,20},{5,21},{6,22},{7,23},{8,24},{9,... | collective-permute-start | bytes 294920 | tf_op jit(solution)/shard_map/ppermute | solution.py:44
  102.5 6.2 %collective-permute-start.7 = (bf16[64,768]{1,0:T(8,128)(2,1)S(1)}, bf16[64,768]{1,0:T(8,128)(2,1)S(1)}, u32[]{:S(2)}, u32[]{:S(2)}) collective-permute-start(bf16[64,768]{1,0:T(8,128)(2,1)S(1)} %get-tuple-element.22), channel_id=1, source_target_pairs={{0,20},{1,21},{2,22},{3,23},{4,24},{5,25},{6,26},{7,27},{8,28},{9,... | collective-permute-start | bytes 294920 | tf_op jit(solution)/shard_map/ppermute | solution.py:44
  108.7 3.9 %collective-permute-start.8 = (bf16[64,768]{1,0:T(8,128)(2,1)S(1)}, bf16[64,768]{1,0:T(8,128)(2,1)S(1)}, u32[]{:S(2)}, u32[]{:S(2)}) collective-permute-start(bf16[64,768]{1,0:T(8,128)(2,1)S(1)} %get-tuple-element.23), channel_id=1, source_target_pairs={{0,24},{1,25},{2,26},{3,27},{4,28},{5,29},{6,30},{7,31},{8,16},{9,... | collective-permute-start | bytes 294920 | tf_op jit(solution)/shard_map/ppermute | solution.py:44
  112.6 4.8 %collective-permute-start.9 = (bf16[64,768]{1,0:T(8,128)(2,1)S(1)}, bf16[64,768]{1,0:T(8,128)(2,1)S(1)}, u32[]{:S(2)}, u32[]{:S(2)}) collective-permute-start(bf16[64,768]{1,0:T(8,128)(2,1)S(1)} %get-tuple-element.24), channel_id=1, source_target_pairs={{0,28},{1,29},{2,30},{3,31},{4,16},{5,17},{6,18},{7,19},{8,20},{9,... | collective-permute-start | bytes 294920 | tf_op jit(solution)/shard_map/ppermute | solution.py:44
  118.8 10.8 %collective-permute-done.8.p2 = bf16[64,768]{1,0:T(8,128)(2,1)S(1)} collective-permute-done((bf16[64,768]{1,0:T(8,128)(2,1)S(1)}, bf16[64,768]{1,0:T(8,128)(2,1)S(1)}, u32[]{:S(2)}, u32[]{:S(2)}) %collective-permute-start.8) | collective-permute-done | bytes 98336 | tf_op jit(solution)/shard_map/ppermute | solution.py:44
  129.7 1.9 %collective-permute-done.9.p3 = bf16[64,768]{1,0:T(8,128)(2,1)S(1)} collective-permute-done((bf16[64,768]{1,0:T(8,128)(2,1)S(1)}, bf16[64,768]{1,0:T(8,128)(2,1)S(1)}, u32[]{:S(2)}, u32[]{:S(2)}) %collective-permute-start.9) | collective-permute-done | bytes 98336 | tf_op jit(solution)/shard_map/ppermute | solution.py:44
  (32 shorter events, 7.0 us)
Async XLA Ops:
  3.2 10.6 %copy-start = (bf16[1,3072,3,128]{3,1,2,0:T(8,128)(2,1)S(1)}, bf16[1,3072,3,128]{3,1,2,0:T(8,128)(2,1)}, u32[]{:S(2)}) copy-start(bf16[1,3072,3,128]{3,1,2,0:T(8,128)(2,1)} %param.9) | copy-start | bytes 7077892
  3.2 51.7 %copy-start.1 = (bf16[1,2048,192]{1,2,0:T(8,128)(2,1)S(1)}, bf16[1,2048,192]{1,2,0:T(8,128)(2,1)}, u32[]{:S(2)}) copy-start(bf16[1,2048,192]{1,2,0:T(8,128)(2,1)} %param.10) | copy-start | bytes 2359300
  3.2 53.6 %copy-start.7 = (f32[1,3,3072]{2,0,1:T(1,128)S(1)}, f32[1,3,3072]{2,0,1:T(1,128)}, u32[]{:S(2)}) copy-start(f32[1,3,3072]{2,0,1:T(1,128)} %param.8) | copy-start | bytes 110596
  3.3 51.7 %all-to-all-start = ((bf16[8,64,3840]{2,1,0:T(8,128)(2,1)}), bf16[8,64,3840]{2,1,0:T(8,128)(2,1)}, u32[]{:S(2)}, u32[]{:S(2)}) async-start(bf16[8,64,3840]{2,1,0:T(8,128)(2,1)} %shard_map.73), calls=%async_computation | async-start | bytes 7864320 | tf_op jit(solution)/shard_map/all_to_all | solution.py:349
  13.8 43.1 %collective-permute-start.1 = (bf16[3,3072,128]{2,1,0:T(8,128)(2,1)S(1)}, bf16[3,3072,128]{2,1,0:T(8,128)(2,1)}, u32[]{:S(2)}, u32[]{:S(2)}) collective-permute-start(bf16[3,3072,128]{2,1,0:T(8,128)(2,1)S(1)} %bitcast.20), channel_id=1, source_target_pairs={{0,1},{1,0},{2,3},{3,2},{4,5},{5,4},{6,7},{7,6},{8,9},{9,8},{10,11... | collective-permute-start | bytes 7077896 | tf_op jit(solution)/shard_map/ppermute | solution.py:32
  54.9 20.2 %collective-permute-start = (bf16[192,2048]{1,0:T(8,128)(2,1)S(1)}, bf16[192,2048]{1,0:T(8,128)(2,1)}, u32[]{:S(2)}, u32[]{:S(2)}) collective-permute-start(bf16[192,2048]{1,0:T(8,128)(2,1)S(1)} %bitcast.22), channel_id=1, source_target_pairs={{0,2},{1,3},{2,0},{3,1},{4,6},{5,7},{6,4},{7,5},{8,10},{9,11},{10,... | collective-permute-start | bytes 2359304 | tf_op jit(solution)/shard_map/ppermute | solution.py:32
  58.6 10.5 %copy-start.8 = (s32[1536]{0:T(1024)S(1)}, s32[1536]{0:T(1024)}, u32[]{:S(2)}) copy-start(s32[1536]{0:T(1024)} %param.13) | copy-start | bytes 18436
  64.7 5.2 %collective-permute-start.2 = (bf16[8,64,384]{2,1,0:T(8,128)(2,1)S(1)}, bf16[8,64,384]{2,1,0:T(8,128)(2,1)S(1)}, u32[]{:S(2)}, u32[]{:S(2)}) collective-permute-start(bf16[8,64,384]{2,1,0:T(8,128)(2,1)S(1)} %get-tuple-element.18), channel_id=1, source_target_pairs={{0,1},{1,0},{2,3},{3,2},{4,5},{5,4},{6,7},{7,6},{8,9},{9,8},{10,11... | collective-permute-start | bytes 1179656 | tf_op jit(solution)/shard_map/ppermute | solution.py:32
  66.7 3.7 %collective-permute-start.3 = (bf16[8,64,384]{2,1,0:T(8,128)(2,1)S(1)}, bf16[8,64,384]{2,1,0:T(8,128)(2,1)S(1)}, u32[]{:S(2)}, u32[]{:S(2)}) collective-permute-start(bf16[8,64,384]{2,1,0:T(8,128)(2,1)S(1)} %get-tuple-element.19), channel_id=1, source_target_pairs={{0,1},{1,0},{2,3},{3,2},{4,5},{5,4},{6,7},{7,6},{8,9},{9,8},{10,11... | collective-permute-start | bytes 1179656 | tf_op jit(solution)/shard_map/ppermute | solution.py:32
  75.1 20.4 %all-to-all-start.1 = ((bf16[16,256,128]{2,1,0:T(8,128)(2,1)}), bf16[16,256,128]{2,1,0:T(8,128)(2,1)}, u32[]{:S(2)}, u32[]{:S(2)}) async-start(bf16[16,256,128]{2,1,0:T(8,128)(2,1)} %bitcast.10), calls=%async_computation.1 | async-start | bytes 2097152 | tf_op jit(solution)/shard_map/all_to_all | solution.py:360
  81.2 5.0 %collective-permute-start.4 = (bf16[192,2048]{1,0:T(8,128)(2,1)S(1)}, bf16[192,2048]{1,0:T(8,128)(2,1)S(1)}, u32[]{:S(2)}, u32[]{:S(2)}) collective-permute-start(bf16[192,2048]{1,0:T(8,128)(2,1)S(1)} %bitcast.23), channel_id=1, source_target_pairs={{0,1},{1,0},{2,3},{3,2},{4,5},{5,4},{6,7},{7,6},{8,9},{9,8},{10,11... | collective-permute-start | bytes 2359304 | tf_op jit(solution)/shard_map/ppermute | solution.py:32
  83.2 4.4 %collective-permute-start.5 = (bf16[192,2048]{1,0:T(8,128)(2,1)}, bf16[192,2048]{1,0:T(8,128)(2,1)S(1)}, u32[]{:S(2)}, u32[]{:S(2)}) collective-permute-start(bf16[192,2048]{1,0:T(8,128)(2,1)} %collective-permute-done.w_y), channel_id=1, source_target_pairs={{0,1},{1,0},{2,3},{3,2},{4,5},{5,4},{6,7},{7,6},{8,9},{9,8},{10,11... | collective-permute-start | bytes 2359304 | tf_op jit(solution)/shard_map/ppermute | solution.py:32
  86.2 0.9 copy-start.3
  87.6 1.0 copy-start.5
  88.6 1.1 copy-start.2
  89.7 1.1 copy-start.4
  90.9 1.1 copy-start.6
  98.2 20.2 %collective-permute-start.6 = (bf16[64,768]{1,0:T(8,128)(2,1)S(1)}, bf16[64,768]{1,0:T(8,128)(2,1)S(1)}, u32[]{:S(2)}, u32[]{:S(2)}) collective-permute-start(bf16[64,768]{1,0:T(8,128)(2,1)S(1)} %get-tuple-element.21), channel_id=1, source_target_pairs={{0,16},{1,17},{2,18},{3,19},{4,20},{5,21},{6,22},{7,23},{8,24},{9,... | collective-permute-start | bytes 294920 | tf_op jit(solution)/shard_map/ppermute | solution.py:44
  102.5 16.3 %collective-permute-start.7 = (bf16[64,768]{1,0:T(8,128)(2,1)S(1)}, bf16[64,768]{1,0:T(8,128)(2,1)S(1)}, u32[]{:S(2)}, u32[]{:S(2)}) collective-permute-start(bf16[64,768]{1,0:T(8,128)(2,1)S(1)} %get-tuple-element.22), channel_id=1, source_target_pairs={{0,20},{1,21},{2,22},{3,23},{4,24},{5,25},{6,26},{7,27},{8,28},{9,... | collective-permute-start | bytes 294920 | tf_op jit(solution)/shard_map/ppermute | solution.py:44
  108.7 20.9 %collective-permute-start.8 = (bf16[64,768]{1,0:T(8,128)(2,1)S(1)}, bf16[64,768]{1,0:T(8,128)(2,1)S(1)}, u32[]{:S(2)}, u32[]{:S(2)}) collective-permute-start(bf16[64,768]{1,0:T(8,128)(2,1)S(1)} %get-tuple-element.23), channel_id=1, source_target_pairs={{0,24},{1,25},{2,26},{3,27},{4,28},{5,29},{6,30},{7,31},{8,16},{9,... | collective-permute-start | bytes 294920 | tf_op jit(solution)/shard_map/ppermute | solution.py:44
  112.6 18.9 %collective-permute-start.9 = (bf16[64,768]{1,0:T(8,128)(2,1)S(1)}, bf16[64,768]{1,0:T(8,128)(2,1)S(1)}, u32[]{:S(2)}, u32[]{:S(2)}) collective-permute-start(bf16[64,768]{1,0:T(8,128)(2,1)S(1)} %get-tuple-element.24), channel_id=1, source_target_pairs={{0,28},{1,29},{2,30},{3,31},{4,16},{5,17},{6,18},{7,19},{8,20},{9,... | collective-permute-start | bytes 294920 | tf_op jit(solution)/shard_map/ppermute | solution.py:44

commit v5 on v4

--- a/solution.py
+++ b/solution.py
@@ -169,13 +169,19 @@
     )(me, gathered, mod, weight)
 
 
-def attend_kernel(me_ref, hide, own, own_old, sib, sib_old, out, query, keys, values, staged, out_sems):
+def attend_kernel(
+    me_ref, hide, own, own_old, sib, sib_far, out, query, keys, values, staged, sib_old, load_sem, out_sems
+):
     _, _, c = place(me_ref)
+    load = pltpu.make_async_copy(sib_far, sib_old, load_sem.at[0])
+    load.start()
     for i, (new, old) in enumerate(((own, own_old), (sib, sib_old))):
         fresh = slice(512 * i, 512 * i + 512)
         query[fresh, :] = new[:, :, 0:128].reshape(512, HD)
         keys[fresh, :] = new[:, :, 128:256].reshape(512, HD)
         values[fresh, 0:128] = new[:, :, 256:384].reshape(512, HD)
+        if i == 1:
+            load.wait()
         for k in range(8):
             at = 1024 + 96 * (8 * i + k)
             keys[at : at + 64, :] = old[k, :, 0:128]
@@ -225,13 +231,15 @@
     return pl.pallas_call(
         attend_kernel,
         out_shape=jax.ShapeDtypeStruct((NX, 4, NX, 64, HD), jnp.bfloat16),
-        in_specs=[SCALAR] + [NEAR] * 5,
+        in_specs=[SCALAR] + [NEAR] * 4 + [FAR],
         out_specs=FAR,
         scratch_shapes=[
             pltpu.VMEM((1024, HD), jnp.bfloat16),
             pltpu.VMEM((2560, HD), jnp.bfloat16),
             pltpu.VMEM((2560, 2 * HD), jnp.bfloat16),
             pltpu.VMEM((NX, 4, NX, 64, HD), jnp.bfloat16),
+            pltpu.VMEM((8, 64, 3 * HD), jnp.bfloat16),
+            pltpu.SemaphoreType.DMA((1,)),
             pltpu.SemaphoreType.DMA((NX,)),
         ],
         compiler_params=params(32),

time: 133 us -> 134 us (level)
  transfers between devices with their start and end apart: 12 -> 12, of which waited for: 8 -> 8; matrix products, arithmetic and copies ran while one was open for 1% -> 1% of each run, Pallas kernels for 10% -> 11%
where the time goes in v5:
time: 134 us; the launch traced here: 133 us
  waiting for transfers between devices  56.5 us (42%)
  starting transfers between devices  48.3 us (36%)
  Pallas kernels  20.8 us (16%)
  local copies, waits for them, and re-layouts  6.17 us (5%)
    all_to_all x1, waiting for transfers between devices, on_device(): lax.all_to_all(sent, 'seq', 0, 0, tiled=True, axis_index_groups=LANES)  39.2 us
    ppermute x4, starting transfers between devices, hand_on(): return lax.ppermute(value, ('pipe', 'seq'), pairs)  19.2 us
    ppermute x4, waiting for transfers between devices, hand_on(): return lax.ppermute(value, ('pipe', 'seq'), pairs)  14.1 us
    ppermute x6, starting transfers between devices, shift(): return lax.ppermute(value, 'seq', pairs)  12.5 us
    all_to_all x1, starting transfers between devices, on_device(): lax.all_to_all(sent, 'seq', 0, 0, tiled=True, axis_index_groups=LANES)  10.6 us
    pallas_call x1, Pallas kernels, project_qkv(): pl.pallas_call(qkv_kernel, out_shape=(shape,) * 4, in_specs=[SCALAR, NEAR...  6.1 us
    all_to_all x1, starting transfers between devices, on_device(): heads = lax.all_to_all(heads.reshape(16, 256, HD), 'seq', 0, 0, tiled=True)  6.08 us
    unnamed x19, local copies, waits for them, and re-layouts  5.28 us
  transfers between devices with their start and end apart: 12, of which 8 were waited for; matrix products, arithmetic and copies ran while one was open for 1% of the time, Pallas kernels for 11%

profile of v5, /device:TPU:6, one launch (start us, length us, event | category | flops | bytes accessed | tf_op | source)
XLA Modules:
  0.0 132.7 jit_solution(1848770759537443494)
XLA Ops:
  0.0 3.2 %shard_map.73 = bf16[8,64,3840]{2,1,0:T(8,128)(2,1)} custom-call(bf16[64,3072]{1,0:T(8,128)(2,1)} %bitcast.28, bf16[192,2048]{1,0:T(8,128)(2,1)} %bitcast.27), custom_call_target="tpu_custom_call" | custom-call | flops 3000000000 | bytes 1 | tf_op jit(solution)/shard_map/pallas_call | solution.py:92
  3.3 10.6 %all-to-all-start = ((bf16[8,64,3840]{2,1,0:T(8,128)(2,1)}), bf16[8,64,3840]{2,1,0:T(8,128)(2,1)}, u32[]{:S(2)}, u32[]{:S(2)}) async-start(bf16[8,64,3840]{2,1,0:T(8,128)(2,1)} %shard_map.73), calls=%async_computation | async-start | bytes 7864320 | tf_op jit(solution)/shard_map/all_to_all | solution.py:357
  13.8 1.9 %collective-permute-start.1 = (bf16[3,3072,128]{2,1,0:T(8,128)(2,1)S(1)}, bf16[3,3072,128]{2,1,0:T(8,128)(2,1)}, u32[]{:S(2)}, u32[]{:S(2)}) collective-permute-start(bf16[3,3072,128]{2,1,0:T(8,128)(2,1)S(1)} %bitcast.20), channel_id=1, source_target_pairs={{0,1},{1,0},{2,3},{3,2},{4,5},{5,4},{6,7},{7,6},{8,9},{9,8},{10,11... | collective-permute-start | bytes 7077896 | tf_op jit(solution)/shard_map/ppermute | solution.py:32
  15.8 39.2 %all-to-all-done.gathered = bf16[8,64,3840]{2,1,0:T(8,128)(2,1)} async-done(((bf16[8,64,3840]{2,1,0:T(8,128)(2,1)}), bf16[8,64,3840]{2,1,0:T(8,128)(2,1)}, u32[]{:S(2)}, u32[]{:S(2)}) %all-to-all-start) | async-done | bytes 3932192 | tf_op jit(solution)/shard_map/all_to_all | solution.py:357
  54.9 1.9 %collective-permute-start = (bf16[192,2048]{1,0:T(8,128)(2,1)S(1)}, bf16[192,2048]{1,0:T(8,128)(2,1)}, u32[]{:S(2)}, u32[]{:S(2)}) collective-permute-start(bf16[192,2048]{1,0:T(8,128)(2,1)S(1)} %bitcast.22), channel_id=1, source_target_pairs={{0,2},{1,3},{2,0},{3,1},{4,6},{5,7},{6,4},{7,5},{8,10},{9,11},{10,... | collective-permute-start | bytes 2359304 | tf_op jit(solution)/shard_map/ppermute | solution.py:32
  56.9 1.7 %shard_map.74.weight = bf16[6,3072,128]{2,1,0:T(8,128)(2,1)S(1)} custom-call(bf16[3,3072,128]{2,1,0:T(8,128)(2,1)S(1)} %bitcast.21, bf16[3,3072,128]{2,1,0:T(8,128)(2,1)} %collective-permute-done.1.w_sib), custom_call_target="tpu_custom_call" | custom-call | flops 10000000 | bytes 1 | tf_op jit(solution)/shard_map/pallas_call | solution.py:119
  58.6 6.1 %shard_map.75 = (bf16[8,64,384]{2,1,0:T(8,128)(2,1)S(1)}, bf16[8,64,384]{2,1,0:T(8,128)(2,1)S(1)}, bf16[8,64,384]{2,1,0:T(8,128)(2,1)S(1)}, bf16[8,64,384]{2,1,0:T(8,128)(2,1)S(1)}) custom-call(s32[1]{0:T(128)} %bitcast.me_ref, bf16[8,64,3840]{2,1,0:T(8,128)(2,1)} %all-to-all-done.gathered, f32[3,3072]{1,0:T(4,128)S(1)} %bitcast.25, ...), custom_call_target="tpu_custom_call" | custom-call | flops 10000000 | bytes 1 | tf_op jit(solution)/shard_map/pallas_call | solution.py:161
  64.7 1.9 %collective-permute-start.2 = (bf16[8,64,384]{2,1,0:T(8,128)(2,1)S(1)}, bf16[8,64,384]{2,1,0:T(8,128)(2,1)S(1)}, u32[]{:S(2)}, u32[]{:S(2)}) collective-permute-start(bf16[8,64,384]{2,1,0:T(8,128)(2,1)S(1)} %get-tuple-element.18), channel_id=1, source_target_pairs={{0,1},{1,0},{2,3},{3,2},{4,5},{5,4},{6,7},{7,6},{8,9},{9,8},{10,11... | collective-permute-start | bytes 1179656 | tf_op jit(solution)/shard_map/ppermute | solution.py:32
  66.7 2.4 %collective-permute-start.3 = (bf16[8,64,384]{2,1,0:T(8,128)(2,1)S(1)}, bf16[8,64,384]{2,1,0:T(8,128)(2,1)S(1)}, u32[]{:S(2)}, u32[]{:S(2)}) collective-permute-start(bf16[8,64,384]{2,1,0:T(8,128)(2,1)S(1)} %get-tuple-element.19), channel_id=1, source_target_pairs={{0,1},{1,0},{2,3},{3,2},{4,5},{5,4},{6,7},{7,6},{8,9},{9,8},{10,11... | collective-permute-start | bytes 1179656 | tf_op jit(solution)/shard_map/ppermute | solution.py:32
  70.4 5.0 %shard_map.76 = bf16[4,4,4,64,128]{4,3,2,1,0:T(8,128)(2,1)} custom-call(s32[1]{0:T(128)} %bitcast.me_ref, f32[1,1536]{1,0:T(1,128)S(1)} %select_n.32.hide, bf16[8,64,384]{2,1,0:T(8,128)(2,1)S(1)} %get-tuple-element.16.own, bf16[8,64,384]{2,1,0:T(8,128)(2,1)S(1)} %get-tuple-element.17.own_old, bf16[8,64,384]{2,1,0:T(8,128)(2,1)S(1)} %collective-permute-done.2.sib, ...), custom_call_target="tpu_custom_call" | custom-call | flops 10000000 | bytes 1 | tf_op jit(solution)/shard_map/pallas_call | solution.py:231
  75.5 6.1 %all-to-all-start.1 = ((bf16[16,256,128]{2,1,0:T(8,128)(2,1)}), bf16[16,256,128]{2,1,0:T(8,128)(2,1)}, u32[]{:S(2)}, u32[]{:S(2)}) async-start(bf16[16,256,128]{2,1,0:T(8,128)(2,1)} %bitcast.10), calls=%async_computation.1 | async-start | bytes 2097152 | tf_op jit(solution)/shard_map/all_to_all | solution.py:368
  81.5 2.0 %collective-permute-start.4 = (bf16[192,2048]{1,0:T(8,128)(2,1)S(1)}, bf16[192,2048]{1,0:T(8,128)(2,1)S(1)}, u32[]{:S(2)}, u32[]{:S(2)}) collective-permute-start(bf16[192,2048]{1,0:T(8,128)(2,1)S(1)} %bitcast.23), channel_id=1, source_target_pairs={{0,1},{1,0},{2,3},{3,2},{4,5},{5,4},{6,7},{7,6},{8,9},{9,8},{10,11... | collective-permute-start | bytes 2359304 | tf_op jit(solution)/shard_map/ppermute | solution.py:32
  83.6 2.3 %collective-permute-start.5 = (bf16[192,2048]{1,0:T(8,128)(2,1)}, bf16[192,2048]{1,0:T(8,128)(2,1)S(1)}, u32[]{:S(2)}, u32[]{:S(2)}) collective-permute-start(bf16[192,2048]{1,0:T(8,128)(2,1)} %collective-permute-done.w_y), channel_id=1, source_target_pairs={{0,1},{1,0},{2,3},{3,2},{4,5},{5,4},{6,7},{7,6},{8,9},{9,8},{10,11... | collective-permute-start | bytes 2359304 | tf_op jit(solution)/shard_map/ppermute | solution.py:32
  89.0 1.1 copy-done.2
  90.1 1.1 copy-done.4
  92.4 1.3 shard_map.77.weight
  93.6 2.2 %all-to-all-done.1.heads = bf16[16,256,128]{2,1,0:T(8,128)(2,1)} async-done(((bf16[16,256,128]{2,1,0:T(8,128)(2,1)}), bf16[16,256,128]{2,1,0:T(8,128)(2,1)}, u32[]{:S(2)}, u32[]{:S(2)}) %all-to-all-start.1) | async-done | bytes 1048608 | tf_op jit(solution)/shard_map/all_to_all | solution.py:368
  95.9 2.7 %shard_map.78 = (bf16[64,768]{1,0:T(8,128)(2,1)S(1)}, bf16[64,768]{1,0:T(8,128)(2,1)S(1)}, bf16[64,768]{1,0:T(8,128)(2,1)S(1)}, bf16[64,768]{1,0:T(8,128)(2,1)S(1)}) custom-call(s32[1]{0:T(128)} %bitcast.me_ref, bf16[16,256,128]{2,1,0:T(8,128)(2,1)} %all-to-all-done.1.heads, bf16[768,2048]{1,0:T(8,128)(2,1)S(1)} %shard_map.77.weight, ...), custom_call_target="tpu_custom_call" | custom-call | flops 2000000000 | bytes 1 | tf_op jit(solution)/shard_map/pallas_call | solution.py:306
  98.6 4.3 %collective-permute-start.6 = (bf16[64,768]{1,0:T(8,128)(2,1)S(1)}, bf16[64,768]{1,0:T(8,128)(2,1)S(1)}, u32[]{:S(2)}, u32[]{:S(2)}) collective-permute-start(bf16[64,768]{1,0:T(8,128)(2,1)S(1)} %get-tuple-element.21), channel_id=1, source_target_pairs={{0,16},{1,17},{2,18},{3,19},{4,20},{5,21},{6,22},{7,23},{8,24},{9,... | collective-permute-start | bytes 294920 | tf_op jit(solution)/shard_map/ppermute | solution.py:44
  102.9 6.2 %collective-permute-start.7 = (bf16[64,768]{1,0:T(8,128)(2,1)S(1)}, bf16[64,768]{1,0:T(8,128)(2,1)S(1)}, u32[]{:S(2)}, u32[]{:S(2)}) collective-permute-start(bf16[64,768]{1,0:T(8,128)(2,1)S(1)} %get-tuple-element.22), channel_id=1, source_target_pairs={{0,20},{1,21},{2,22},{3,23},{4,24},{5,25},{6,26},{7,27},{8,28},{9,... | collective-permute-start | bytes 294920 | tf_op jit(solution)/shard_map/ppermute | solution.py:44
  109.1 3.9 %collective-permute-start.8 = (bf16[64,768]{1,0:T(8,128)(2,1)S(1)}, bf16[64,768]{1,0:T(8,128)(2,1)S(1)}, u32[]{:S(2)}, u32[]{:S(2)}) collective-permute-start(bf16[64,768]{1,0:T(8,128)(2,1)S(1)} %get-tuple-element.23), channel_id=1, source_target_pairs={{0,24},{1,25},{2,26},{3,27},{4,28},{5,29},{6,30},{7,31},{8,16},{9,... | collective-permute-start | bytes 294920 | tf_op jit(solution)/shard_map/ppermute | solution.py:44
  113.0 4.8 %collective-permute-start.9 = (bf16[64,768]{1,0:T(8,128)(2,1)S(1)}, bf16[64,768]{1,0:T(8,128)(2,1)S(1)}, u32[]{:S(2)}, u32[]{:S(2)}) collective-permute-start(bf16[64,768]{1,0:T(8,128)(2,1)S(1)} %get-tuple-element.24), channel_id=1, source_target_pairs={{0,28},{1,29},{2,30},{3,31},{4,16},{5,17},{6,18},{7,19},{8,20},{9,... | collective-permute-start | bytes 294920 | tf_op jit(solution)/shard_map/ppermute | solution.py:44
  119.2 10.8 %collective-permute-done.8.p2 = bf16[64,768]{1,0:T(8,128)(2,1)S(1)} collective-permute-done((bf16[64,768]{1,0:T(8,128)(2,1)S(1)}, bf16[64,768]{1,0:T(8,128)(2,1)S(1)}, u32[]{:S(2)}, u32[]{:S(2)}) %collective-permute-start.8) | collective-permute-done | bytes 98336 | tf_op jit(solution)/shard_map/ppermute | solution.py:44
  130.0 1.9 %collective-permute-done.9.p3 = bf16[64,768]{1,0:T(8,128)(2,1)S(1)} collective-permute-done((bf16[64,768]{1,0:T(8,128)(2,1)S(1)}, bf16[64,768]{1,0:T(8,128)(2,1)S(1)}, u32[]{:S(2)}, u32[]{:S(2)}) %collective-permute-start.9) | collective-permute-done | bytes 98336 | tf_op jit(solution)/shard_map/ppermute | solution.py:44
  (32 shorter events, 7.0 us)
Async XLA Ops:
  3.2 10.6 %copy-start = (bf16[1,3072,3,128]{3,1,2,0:T(8,128)(2,1)S(1)}, bf16[1,3072,3,128]{3,1,2,0:T(8,128)(2,1)}, u32[]{:S(2)}) copy-start(bf16[1,3072,3,128]{3,1,2,0:T(8,128)(2,1)} %param.9) | copy-start | bytes 7077892
  3.2 51.7 %copy-start.1 = (bf16[1,2048,192]{1,2,0:T(8,128)(2,1)S(1)}, bf16[1,2048,192]{1,2,0:T(8,128)(2,1)}, u32[]{:S(2)}) copy-start(bf16[1,2048,192]{1,2,0:T(8,128)(2,1)} %param.10) | copy-start | bytes 2359300
  3.2 53.6 %copy-start.7 = (f32[1,3,3072]{2,0,1:T(1,128)S(1)}, f32[1,3,3072]{2,0,1:T(1,128)}, u32[]{:S(2)}) copy-start(f32[1,3,3072]{2,0,1:T(1,128)} %param.8) | copy-start | bytes 110596
  3.3 51.7 %all-to-all-start = ((bf16[8,64,3840]{2,1,0:T(8,128)(2,1)}), bf16[8,64,3840]{2,1,0:T(8,128)(2,1)}, u32[]{:S(2)}, u32[]{:S(2)}) async-start(bf16[8,64,3840]{2,1,0:T(8,128)(2,1)} %shard_map.73), calls=%async_computation | async-start | bytes 7864320 | tf_op jit(solution)/shard_map/all_to_all | solution.py:357
  13.8 43.1 %collective-permute-start.1 = (bf16[3,3072,128]{2,1,0:T(8,128)(2,1)S(1)}, bf16[3,3072,128]{2,1,0:T(8,128)(2,1)}, u32[]{:S(2)}, u32[]{:S(2)}) collective-permute-start(bf16[3,3072,128]{2,1,0:T(8,128)(2,1)S(1)} %bitcast.20), channel_id=1, source_target_pairs={{0,1},{1,0},{2,3},{3,2},{4,5},{5,4},{6,7},{7,6},{8,9},{9,8},{10,11... | collective-permute-start | bytes 7077896 | tf_op jit(solution)/shard_map/ppermute | solution.py:32
  54.9 20.5 %collective-permute-start = (bf16[192,2048]{1,0:T(8,128)(2,1)S(1)}, bf16[192,2048]{1,0:T(8,128)(2,1)}, u32[]{:S(2)}, u32[]{:S(2)}) collective-permute-start(bf16[192,2048]{1,0:T(8,128)(2,1)S(1)} %bitcast.22), channel_id=1, source_target_pairs={{0,2},{1,3},{2,0},{3,1},{4,6},{5,7},{6,4},{7,5},{8,10},{9,11},{10,... | collective-permute-start | bytes 2359304 | tf_op jit(solution)/shard_map/ppermute | solution.py:32
  58.6 10.5 %copy-start.8 = (s32[1536]{0:T(1024)S(1)}, s32[1536]{0:T(1024)}, u32[]{:S(2)}) copy-start(s32[1536]{0:T(1024)} %param.13) | copy-start | bytes 18436
  64.7 5.2 %collective-permute-start.2 = (bf16[8,64,384]{2,1,0:T(8,128)(2,1)S(1)}, bf16[8,64,384]{2,1,0:T(8,128)(2,1)S(1)}, u32[]{:S(2)}, u32[]{:S(2)}) collective-permute-start(bf16[8,64,384]{2,1,0:T(8,128)(2,1)S(1)} %get-tuple-element.18), channel_id=1, source_target_pairs={{0,1},{1,0},{2,3},{3,2},{4,5},{5,4},{6,7},{7,6},{8,9},{9,8},{10,11... | collective-permute-start | bytes 1179656 | tf_op jit(solution)/shard_map/ppermute | solution.py:32
  66.7 3.7 %collective-permute-start.3 = (bf16[8,64,384]{2,1,0:T(8,128)(2,1)S(1)}, bf16[8,64,384]{2,1,0:T(8,128)(2,1)S(1)}, u32[]{:S(2)}, u32[]{:S(2)}) collective-permute-start(bf16[8,64,384]{2,1,0:T(8,128)(2,1)S(1)} %get-tuple-element.19), channel_id=1, source_target_pairs={{0,1},{1,0},{2,3},{3,2},{4,5},{5,4},{6,7},{7,6},{8,9},{9,8},{10,11... | collective-permute-start | bytes 1179656 | tf_op jit(solution)/shard_map/ppermute | solution.py:32
  75.5 20.4 %all-to-all-start.1 = ((bf16[16,256,128]{2,1,0:T(8,128)(2,1)}), bf16[16,256,128]{2,1,0:T(8,128)(2,1)}, u32[]{:S(2)}, u32[]{:S(2)}) async-start(bf16[16,256,128]{2,1,0:T(8,128)(2,1)} %bitcast.10), calls=%async_computation.1 | async-start | bytes 2097152 | tf_op jit(solution)/shard_map/all_to_all | solution.py:368
  81.5 5.0 %collective-permute-start.4 = (bf16[192,2048]{1,0:T(8,128)(2,1)S(1)}, bf16[192,2048]{1,0:T(8,128)(2,1)S(1)}, u32[]{:S(2)}, u32[]{:S(2)}) collective-permute-start(bf16[192,2048]{1,0:T(8,128)(2,1)S(1)} %bitcast.23), channel_id=1, source_target_pairs={{0,1},{1,0},{2,3},{3,2},{4,5},{5,4},{6,7},{7,6},{8,9},{9,8},{10,11... | collective-permute-start | bytes 2359304 | tf_op jit(solution)/shard_map/ppermute | solution.py:32
  83.6 4.4 %collective-permute-start.5 = (bf16[192,2048]{1,0:T(8,128)(2,1)}, bf16[192,2048]{1,0:T(8,128)(2,1)S(1)}, u32[]{:S(2)}, u32[]{:S(2)}) collective-permute-start(bf16[192,2048]{1,0:T(8,128)(2,1)} %collective-permute-done.w_y), channel_id=1, source_target_pairs={{0,1},{1,0},{2,3},{3,2},{4,5},{5,4},{6,7},{7,6},{8,9},{9,8},{10,11... | collective-permute-start | bytes 2359304 | tf_op jit(solution)/shard_map/ppermute | solution.py:32
  86.6 0.9 copy-start.3
  88.0 1.0 copy-start.5
  89.0 1.1 copy-start.2
  90.1 1.1 copy-start.4
  91.2 1.1 copy-start.6
  98.6 20.2 %collective-permute-start.6 = (bf16[64,768]{1,0:T(8,128)(2,1)S(1)}, bf16[64,768]{1,0:T(8,128)(2,1)S(1)}, u32[]{:S(2)}, u32[]{:S(2)}) collective-permute-start(bf16[64,768]{1,0:T(8,128)(2,1)S(1)} %get-tuple-element.21), channel_id=1, source_target_pairs={{0,16},{1,17},{2,18},{3,19},{4,20},{5,21},{6,22},{7,23},{8,24},{9,... | collective-permute-start | bytes 294920 | tf_op jit(solution)/shard_map/ppermute | solution.py:44
  102.9 16.3 %collective-permute-start.7 = (bf16[64,768]{1,0:T(8,128)(2,1)S(1)}, bf16[64,768]{1,0:T(8,128)(2,1)S(1)}, u32[]{:S(2)}, u32[]{:S(2)}) collective-permute-start(bf16[64,768]{1,0:T(8,128)(2,1)S(1)} %get-tuple-element.22), channel_id=1, source_target_pairs={{0,20},{1,21},{2,22},{3,23},{4,24},{5,25},{6,26},{7,27},{8,28},{9,... | collective-permute-start | bytes 294920 | tf_op jit(solution)/shard_map/ppermute | solution.py:44
  109.1 20.9 %collective-permute-start.8 = (bf16[64,768]{1,0:T(8,128)(2,1)S(1)}, bf16[64,768]{1,0:T(8,128)(2,1)S(1)}, u32[]{:S(2)}, u32[]{:S(2)}) collective-permute-start(bf16[64,768]{1,0:T(8,128)(2,1)S(1)} %get-tuple-element.23), channel_id=1, source_target_pairs={{0,24},{1,25},{2,26},{3,27},{4,28},{5,29},{6,30},{7,31},{8,16},{9,... | collective-permute-start | bytes 294920 | tf_op jit(solution)/shard_map/ppermute | solution.py:44
  113.0 18.9 %collective-permute-start.9 = (bf16[64,768]{1,0:T(8,128)(2,1)S(1)}, bf16[64,768]{1,0:T(8,128)(2,1)S(1)}, u32[]{:S(2)}, u32[]{:S(2)}) collective-permute-start(bf16[64,768]{1,0:T(8,128)(2,1)S(1)} %get-tuple-element.24), channel_id=1, source_target_pairs={{0,28},{1,29},{2,30},{3,31},{4,16},{5,17},{6,18},{7,19},{8,20},{9,... | collective-permute-start | bytes 294920 | tf_op jit(solution)/shard_map/ppermute | solution.py:44
